TPU v7x, 32 devices: a whole 2x2x4 slice. The times are simulated.
32 devices in a mesh: sector: 4 (over y, core), axial: 8 (over z, x).
Axes of the slice: x: 2, y: 2, z: 4, core: 2. Of those that a mesh axis runs over, the one named last changes fastest.
Arguments:
- adjoint: float32 [5, 64, 32768], P(None, None, ('sector', 'axial')), may hold values from -6 to 6
- velocity: bfloat16 [3, 64, 32768], P(None, None, ('sector', 'axial')), may hold values from -6 to 6
- drag: float32 [32768], P(('sector', 'axial')), may hold values from 0.5 to 5
- block_weight: float32 [32768], P(('sector', 'axial')), may hold values from 0.2 to 1
- flux_jac: float32 [3, 5, 5], replicated, may hold values from -2.5 to 2.5
- face_own: float32 [6, 5, 5], replicated, may hold values from -4 to 4
- face_nbr: float32 [6, 5, 5], replicated, may hold values from -4 to 4
- nbr_local: int32 [6, 32768], P(None, ('sector', 'axial')), may hold values from 0 to 1024, as said below
- sector_slots: int32 [2, 8192], P(None, ('sector', 'axial')), may hold values from 0 to 1023, as said below
- axial_slots: int32 [2, 8192], P(None, ('sector', 'axial')), may hold values from 0 to 1023, as said below
- sector_live: int32 [4, 8, 2], P('sector', 'axial'), may hold values from 128 to 256, as said below
- elem_block: int32 [32768], P(('sector', 'axial')), may hold values from 0 to 4095, as said below
Outputs:
- adjoint_next: float32 [5, 64, 32768], P(None, None, ('sector', 'axial'))
- block_grad: float32 [4096], P(('sector', 'axial'))
Inputs may be any that keep to these rules, and one draw needn't show every extreme that they name: The elements of one device fill a block of 4 x 64 x 4 cells in some order; nbr_local is symmetric: across face f of element e lies face f xor 1 of element nbr_local[f, e]; the value 1024 marks faces on the device boundary. `sector_slots`: each row lists 256 distinct local elements of the device; slot s of one device's upper row and slot s of the next device's lower row are the two sides of one face with matching node order. `axial_slots`: each row lists 256 distinct local elements of the device; slot s of one device's upper row and slot s of the next slab's lower row are the two sides of one face with matching node order. `sector_live`: A device's upper count equals the lower count of the device one higher in sector index (cyclically). `elem_block`: the owner of an element's block (block // 128, in joint device order) is the element's own device or the one just before or after it, cyclically.
All inputs are finite; a program needn't handle non-finite values.
Results may differ from a plain program's by a relative error of at most 0.0006.
Values sent between devices are 32-bit elements; how exact they have to be, the bound alone decides.
A program may use at most 128 MiB of HBM per device.

v0:
```python
import functools

import jax
import jax.numpy as jnp
import numpy as np
from jax import lax
from jax.experimental import pallas as pl
from jax.experimental.pallas import tpu as pltpu
from jax.sharding import PartitionSpec as P

BLOCKS = 4096
BF = jnp.bfloat16
F32 = jnp.float32
MESH = pl.DeviceIdType.MESH
INPUTS = 15


def lobatto_tables():
    points = np.array([-1.0, -1.0 / np.sqrt(5.0), 1.0 / np.sqrt(5.0), 1.0])
    weights = np.array([1.0, 5.0, 5.0, 1.0]) / 6.0
    scales = np.array(
        [np.prod([points[i] - points[k] for k in range(4) if k != i]) for i in range(4)]
    )
    derivative = np.zeros((4, 4))
    for i in range(4):
        for p in range(4):
            if i != p:
                derivative[i, p] = scales[i] / scales[p] / (points[i] - points[p])
            else:
                derivative[i, p] = sum((1.0 / (points[i] - points[k]) for k in range(4) if k != i))
    node_weight = (
        weights[:, None, None] * weights[None, :, None] * weights[None, None, :]
    ).reshape(64) / 8.0
    return (derivative, node_weight)


def constant_tables():
    derivative, node_weight = lobatto_tables()
    eye = np.eye(4)
    step = derivative.T
    along = [
        np.kron(np.kron(step, eye), eye),
        np.kron(np.kron(eye, step), eye),
        np.kron(np.kron(eye, eye), step),
    ]
    nodes = np.arange(64).reshape(4, 4, 4)
    faces = [nodes[0], nodes[3], nodes[:, 0], nodes[:, 3], nodes[:, :, 0], nodes[:, :, 3]]
    faces = [f.reshape(16) for f in faces]
    mats = list(along)
    pick = np.zeros((96, 64))
    lift = np.zeros((64, 512))
    for f, ids in enumerate(faces):
        diag = np.zeros((64, 64))
        diag[ids, ids] = 1.0
        mats.append(diag)
        pick[16 * f + np.arange(16), ids] = 1.0
        for h in range(5):
            lift[ids, 80 * f + 16 * h + np.arange(16)] = 0.1
    mats = [0.1 * np.concatenate([m, m], axis=1) for m in mats]
    mats.append(np.repeat(node_weight[:, None], 128, axis=1))
    return (
        jnp.asarray(np.stack(mats), F32),
        jnp.asarray(pick, BF),
        jnp.asarray(lift, F32),
    )


def split2(x):
    hi = x.astype(BF)
    return hi, (x - hi.astype(F32)).astype(BF)


def dot(a, b):
    return jnp.dot(a, b, preferred_element_type=F32)


def dot_nt(a, b):
    return lax.dot_general(a, b, (((1,), (1,)), ((), ())), preferred_element_type=F32)


def one_hot(mask):
    return jnp.where(mask, 1.0, 0.0).astype(BF)


def kernel(
    sectors,
    slabs,
    owned,
    *refs,
):
    hbm_refs = refs[:INPUTS]
    out_ref, grad_ref = refs[INPUTS : INPUTS + 2]
    vmem_refs = refs[INPUTS + 2 : 2 * INPUTS + 2]
    rest_refs = refs[2 * INPUTS + 2 :]
    (
        x_ref,
        vel_ref,
        drag_ref,
        bw_ref,
        jac_ref,
        own_ref,
        nbrmat_ref,
        nbr_ref,
        sslots_ref,
        aslots_ref,
        live_ref,
        eb_ref,
        mats_ref,
        pick_ref,
        lift_ref,
    ) = vmem_refs
    (
        xs_ref,
        tr_ref,
        oh_ref,
        send_ref,
        recv_ref,
        part_ref,
        ps_ref,
        a_ref,
        b_ref,
        bsend_ref,
        brecv_ref,
        send_sem,
        recv_sem,
        load_sem,
    ) = rest_refs
    loads = {
        k: pltpu.make_async_copy(hbm_refs[k], vmem_refs[k], load_sem.at[k])
        for k in range(1, INPUTS)
    }
    fields = [
        pltpu.make_async_copy(hbm_refs[0].at[h], x_ref.at[h], load_sem.at[INPUTS + h])
        for h in range(5)
    ]
    for k in (8, 9, 4, 5, 6, 12, 14, 13):
        loads[k].start()
    for field in fields:
        field.start()
    for k in (1, 2, 3, 11, 7, 10):
        loads[k].start()
    elems = x_ref.shape[2]
    slots = sslots_ref.shape[1]
    width = bsend_ref.shape[2]
    count = sectors * slabs
    sec = lax.axis_index("sector")
    axi = lax.axis_index("axial")
    joint = sec * slabs + axi
    prev = lax.rem(joint + count - 1, count)
    nxt = lax.rem(joint + 1, count)
    dev_prev = (prev // slabs, lax.rem(prev, slabs))
    dev_next = (nxt // slabs, lax.rem(nxt, slabs))
    dev_low = (lax.rem(sec + sectors - 1, sectors), axi)
    dev_high = (lax.rem(sec + 1, sectors), axi)

    barrier = pltpu.get_barrier_semaphore()
    for device in (dev_prev, dev_next, dev_low, dev_high):
        pl.semaphore_signal(barrier, inc=1, device_id=device, device_id_type=MESH)

    loads[8].wait()
    loads[9].wait()
    rows_slots = lax.broadcasted_iota(jnp.int32, (elems, slots), 0)
    sides = ((0, sslots_ref, 0), (1, sslots_ref, 1), (4, aslots_ref, 0), (5, aslots_ref, 1))
    for i, (face, ref, row) in enumerate(sides):
        oh_ref[i] = one_hot(rows_slots == ref[row : row + 1, :])

    for k in (4, 5, 6, 12, 14):
        loads[k].wait()
    spread = lax.broadcasted_iota(jnp.int32, (5, 384), 1) // 64
    spread = jnp.where(spread == lax.broadcasted_iota(jnp.int32, (5, 384), 0), 1.0, 0.0)
    lane = lax.broadcasted_iota(jnp.int32, (6, 512), 1)
    face_row = lax.broadcasted_iota(jnp.int32, (6, 512), 0)
    slot_row = lane // 16 - 5 * face_row
    for c in range(5):
        rows = slice(64 * c, 64 * c + 64)
        jac = jac_ref[0][:, c : c + 1] * spread[0:1, :]
        face = own_ref[c][:, 0:1] * spread[0:1, :]
        nbrs = jnp.where(slot_row == 0, nbrmat_ref[c][:, 0:1], 0.0)
        for h in range(1, 5):
            jac += jac_ref[h][:, c : c + 1] * spread[h : h + 1, :]
            face += own_ref[c][:, h : h + 1] * spread[h : h + 1, :]
            nbrs = jnp.where(slot_row == h, nbrmat_ref[c][:, h : h + 1], nbrs)
        rown = jnp.sum(nbrs, axis=0, keepdims=True)
        for t in range(3):
            lanes = slice(128 * t, 128 * t + 128)
            total = mats_ref[0] * jac[0:1, lanes]
            for j in range(1, 9):
                row = jac[j : j + 1, lanes] if j < 3 else face[j - 3 : j - 2, lanes]
                total += mats_ref[j] * row
            hi, lo = split2(total)
            for base, part in ((0, hi), (384, hi), (768, lo)):
                a_ref[rows, base + 128 * t : base + 128 * t + 128] = part
        hi, lo = split2(lift_ref[...] * rown)
        b_ref[rows, 0:512] = hi
        b_ref[rows, 512:1024] = hi
        b_ref[rows, 1024:1536] = lo

    loads[13].wait()
    for h in range(5):
        fields[h].wait()
        hi, lo = split2(x_ref[h])
        for base, part in ((0, hi), (384, lo), (768, hi)):
            xs_ref[base + 64 * h : base + 64 * h + 64, :] = part
        for s, half in enumerate((hi, lo)):
            picked = dot(pick_ref[...], half).astype(BF)
            for f in range(6):
                row = 80 * s + 16 * h
                tr_ref[f, row : row + 16, :] = picked[16 * f : 16 * f + 16, :]
    for base in (320, 704, 1088):
        xs_ref[base : base + 64, :] = jnp.zeros((64, elems), BF)

    for i, face in enumerate((0, 1, 4, 5)):
        both = dot(tr_ref[face], oh_ref[i])
        send_ref[i] = both[:80] + both[80:]

    pl.semaphore_wait(barrier, 4)

    def remote(src, dst, k, device):
        return pltpu.make_async_remote_copy(
            src_ref=src,
            dst_ref=dst,
            send_sem=send_sem.at[k],
            recv_sem=recv_sem.at[k],
            device_id=device,
            device_id_type=MESH,
        )

    up_x = remote(send_ref.at[1], recv_ref.at[0], 0, dev_high)
    down_x = remote(send_ref.at[0], recv_ref.at[1], 1, dev_low)
    up_z = remote(send_ref.at[3], recv_ref.at[2], 2, dev_next)
    down_z = remote(send_ref.at[2], recv_ref.at[3], 3, dev_prev)
    up_b = remote(bsend_ref.at[2], brecv_ref.at[0], 4, dev_next)
    down_b = remote(bsend_ref.at[0], brecv_ref.at[1], 5, dev_prev)
    has_low = axi > 0
    has_high = axi < slabs - 1
    up_x.start()
    down_x.start()

    @pl.when(has_high)
    def _():
        up_z.start()

    @pl.when(has_low)
    def _():
        down_z.start()

    @pl.when(jnp.logical_not(has_low))
    def _():
        recv_ref[2] = jnp.zeros((80, slots), F32)

    @pl.when(jnp.logical_not(has_high))
    def _():
        recv_ref[3] = jnp.zeros((80, slots), F32)

    for k in (1, 2, 3, 11):
        loads[k].wait()
    drag = drag_ref[...]
    acc = x_ref[1] * vel_ref[0].astype(F32)
    acc += x_ref[2] * vel_ref[1].astype(F32)
    acc += x_ref[3] * vel_ref[2].astype(F32)
    elem_grad = drag * jnp.sum(acc * mats_ref[9][:, 0:1], axis=0, keepdims=True)
    weighted = bw_ref[...] * elem_grad
    w1 = weighted.astype(BF)
    rest = weighted - w1.astype(F32)
    w2 = rest.astype(BF)
    w3 = (rest - w2.astype(F32)).astype(BF).astype(F32)
    row16 = lax.broadcasted_iota(jnp.int32, (16, elems), 0)
    stack = jnp.where(row16 == 0, w1.astype(F32), 0.0)
    stack = jnp.where(row16 == 1, w2.astype(F32), stack)
    stack = jnp.where(row16 == 2, w3, stack).astype(BF)
    rel = eb_ref[...] - (joint - 1) * owned
    rel = jnp.where(rel < 0, rel + BLOCKS, rel)
    rel = jnp.where(rel >= BLOCKS, rel - BLOCKS, rel)
    rows_blk = lax.broadcasted_iota(jnp.int32, (width, elems), 0)
    for j in range(3):
        sums = dot_nt(stack, one_hot(rows_blk == rel - j * owned))
        total = jnp.sum(sums, axis=0, keepdims=True)
        bsend_ref[j] = jnp.broadcast_to(total, (8, width))
    up_b.start()
    down_b.start()

    own = dot(a_ref[...], xs_ref[...])
    keep = 1.0 - 0.1 * drag
    for c in range(5):
        x = x_ref[c]
        scaled = x * keep if 1 <= c <= 3 else x
        out_ref[c] = scaled + own[64 * c : 64 * c + 64, :]

    loads[7].wait()
    chunk = 256
    rows_src = lax.broadcasted_iota(jnp.int32, (chunk, elems), 0)

    def gather(f, carry):
        ids = nbr_ref[pl.ds(f, 1), :]
        g = f + 1 - 2 * lax.rem(f, 2)
        both = jnp.zeros((160, elems), F32)
        for k in range(elems // chunk):
            hot = one_hot(rows_src == ids - k * chunk)
            both += dot(tr_ref[g, :, k * chunk : (k + 1) * chunk], hot)
        part_ref[f] = both[:80] + both[80:]
        return carry

    lax.fori_loop(0, 6, gather, 0)

    def put_partner(face, value):
        hi, lo = split2(value)
        for base, part in ((0, hi), (512, lo), (1024, hi)):
            ps_ref[base + 80 * face : base + 80 * face + 80, :] = part

    put_partner(2, part_ref[2])
    put_partner(3, part_ref[3])
    for base in (480, 992, 1504):
        ps_ref[base : base + 32, :] = jnp.zeros((32, elems), BF)

    up_x.wait()
    down_x.wait()

    @pl.when(has_high)
    def _():
        up_z.wait_send()
        down_z.wait_recv()

    @pl.when(has_low)
    def _():
        down_z.wait_send()
        up_z.wait_recv()

    loads[10].wait()
    slot_ids = lax.broadcasted_iota(jnp.int32, (80, slots), 1)
    for i, face in enumerate((0, 1, 4, 5)):
        got = recv_ref[i]
        if i < 2:
            got = jnp.where(slot_ids < live_ref[:, i : i + 1], got, 0.0)
        both = dot_nt(jnp.concatenate(split2(got), axis=0), oh_ref[i])
        put_partner(face, part_ref[face] + (both[:80] + both[80:]))
    nbr = dot(b_ref[...], ps_ref[...])
    for c in range(5):
        out_ref[c] += nbr[64 * c : 64 * c + 64, :]

    up_b.wait()
    down_b.wait()
    sums = bsend_ref[1] + brecv_ref[0] + brecv_ref[1]
    grad_ref[...] = sums[0, :owned]


def on_device(
    sectors,
    slabs,
    adjoint,
    velocity,
    drag,
    block_weight,
    flux_jac,
    face_own,
    face_nbr,
    nbr_local,
    sector_slots,
    axial_slots,
    sector_live,
    elem_block,
):
    elems = adjoint.shape[2]
    slots = sector_slots.shape[1]
    owned = BLOCKS // (sectors * slabs)
    width = -(-owned // 128) * 128
    operands = (
        adjoint,
        velocity,
        drag.reshape(1, elems),
        block_weight.reshape(1, elems),
        jnp.transpose(flux_jac, (1, 0, 2)),
        jnp.transpose(face_own, (1, 0, 2)),
        jnp.transpose(face_nbr, (1, 0, 2)),
        nbr_local,
        sector_slots,
        axial_slots,
        sector_live.reshape(1, 2),
        elem_block.reshape(1, elems),
        *constant_tables(),
    )
    vmem = pl.BlockSpec(memory_space=pltpu.VMEM)
    hbm = pl.BlockSpec(memory_space=pltpu.HBM)
    out, grad = pl.pallas_call(
        functools.partial(kernel, sectors, slabs, owned),
        out_shape=(
            pltpu.VMEM(adjoint.shape, F32),
            pltpu.VMEM((owned,), F32),
        ),
        in_specs=[hbm] * INPUTS,
        out_specs=(vmem, vmem),
        scratch_shapes=[pltpu.VMEM(a.shape, a.dtype) for a in operands]
        + [
            pltpu.VMEM((1152, elems), BF),
            pltpu.VMEM((6, 160, elems), BF),
            pltpu.VMEM((4, elems, slots), BF),
            pltpu.VMEM((4, 80, slots), F32),
            pltpu.VMEM((4, 80, slots), F32),
            pltpu.VMEM((6, 80, elems), F32),
            pltpu.VMEM((1536, elems), BF),
            pltpu.VMEM((320, 1152), BF),
            pltpu.VMEM((320, 1536), BF),
            pltpu.VMEM((3, 8, width), F32),
            pltpu.VMEM((2, 8, width), F32),
            pltpu.SemaphoreType.DMA((6,)),
            pltpu.SemaphoreType.DMA((6,)),
            pltpu.SemaphoreType.DMA((INPUTS + 5,)),
        ],
        compiler_params=pltpu.CompilerParams(
            collective_id=0, has_side_effects=True, vmem_limit_bytes=60 * 1024 * 1024
        ),
    )(*operands)
    return out, grad


def solution(mesh):
    placed = (
        P(None, None, ("sector", "axial")),
        P(None, None, ("sector", "axial")),
        P(("sector", "axial")),
        P(("sector", "axial")),
        P(),
        P(),
        P(),
        P(None, ("sector", "axial")),
        P(None, ("sector", "axial")),
        P(None, ("sector", "axial")),
        P("sector", "axial", None),
        P(("sector", "axial")),
    )
    return jax.shard_map(
        functools.partial(on_device, mesh.shape["sector"], mesh.shape["axial"]),
        mesh=mesh,
        in_specs=placed,
        out_specs=(P(None, None, ("sector", "axial")), P(("sector", "axial"))),
        check_vma=False,
    )
```

profile of v0, /device:TPU:0, one launch (start us, length us, event | category | flops | bytes accessed | tf_op | source)
XLA Modules:
  0.0 15.7 jit_solution(14525376047919720190)
XLA Ops:
  0.6 13.5 %shard_map.158 = (f32[5,64,1024]{2,1,0:T(8,128)S(1)}, f32[128]{0:T(128)S(1)}) custom-call(f32[5,64,1024]{2,1,0:T(8,128)} %refs_0_.1, bf16[3,64,1024]{2,1,0:T(8,128)(2,1)} %refs_1_.1, f32[1,1024]{1,0:T(1,128)} %bitcast.10, f32[1,1024]{1,0:T(1,128)} %bitcast.11, f32[5,3,5]{2,1,0:T(4,128)} %bitcast.9, f32[5,6,5]{2,1,0:T(8,128)} %bitcast.7, f32[5,6,5]{2,1,0:T(8,128)} %bitcast.8, ...), custom_call_target="tpu_custom_call" | custom-call | tf_op jit(solution)/shard_map/pallas_call | solution.py:383
  14.1 1.1 %copy.19 = f32[5,64,1024]{2,1,0:T(8,128)} copy(f32[5,64,1024]{2,1,0:T(8,128)S(1)} %get-tuple-element.2) | data formatting | bytes 2621440
  15.2 0.5 %copy.20 = f32[128]{0:T(128)} copy(f32[128]{0:T(128)S(1)} %get-tuple-element.3) | data formatting | bytes 1024
where the time goes:
time: 15.9 us; the launch traced here: 15.7 us
  Pallas kernels  13.5 us (85%)
  local copies, waits for them, and re-layouts  1.57 us (10%)
  between operations  0.64 us (4%)
    pallas_call x1, Pallas kernels, on_device(): pl.pallas_call(functools.partial(kernel, sectors, slabs, owned), out_shap...  13.5 us
    unnamed x2, local copies, waits for them, and re-layouts  1.57 us

commit v1 on v0

v1 whole, which is shorter than its diff:
```python
import functools

import jax
import jax.numpy as jnp
import numpy as np
from jax import lax
from jax.experimental import pallas as pl
from jax.experimental.pallas import tpu as pltpu
from jax.sharding import PartitionSpec as P

BLOCKS = 4096
BF = jnp.bfloat16
F32 = jnp.float32
MESH = pl.DeviceIdType.MESH
INPUTS = 13
SIDES = (0, 1, 4, 5)


def lobatto_tables():
    points = np.array([-1.0, -1.0 / np.sqrt(5.0), 1.0 / np.sqrt(5.0), 1.0])
    weights = np.array([1.0, 5.0, 5.0, 1.0]) / 6.0
    scales = np.array(
        [np.prod([points[i] - points[k] for k in range(4) if k != i]) for i in range(4)]
    )
    derivative = np.zeros((4, 4))
    for i in range(4):
        for p in range(4):
            if i != p:
                derivative[i, p] = scales[i] / scales[p] / (points[i] - points[p])
            else:
                derivative[i, p] = sum((1.0 / (points[i] - points[k]) for k in range(4) if k != i))
    node_weight = (
        weights[:, None, None] * weights[None, :, None] * weights[None, None, :]
    ).reshape(64) / 8.0
    return (derivative, node_weight)


def constant_tables():
    derivative, node_weight = lobatto_tables()
    eye = np.eye(4)
    step = derivative.T
    mats = [
        np.kron(np.kron(step, eye), eye),
        np.kron(np.kron(eye, step), eye),
        np.kron(np.kron(eye, eye), step),
    ]
    nodes = np.arange(64).reshape(4, 4, 4)
    faces = [nodes[0], nodes[3], nodes[:, 0], nodes[:, 3], nodes[:, :, 0], nodes[:, :, 3]]
    for ids in faces:
        diag = np.zeros((64, 64))
        diag[ids.reshape(16), ids.reshape(16)] = 1.0
        mats.append(diag)
    mats = [0.1 * np.concatenate([m, m], axis=1) for m in mats]
    mats.append(np.repeat(node_weight[:, None], 128, axis=1))
    return jnp.asarray(np.stack(mats), F32)


def split2(x):
    hi = x.astype(BF)
    return hi, (x - hi.astype(F32)).astype(BF)


def dot(a, b):
    return jnp.dot(a, b, preferred_element_type=F32)


def dot_nt(a, b):
    return lax.dot_general(a, b, (((1,), (1,)), ((), ())), preferred_element_type=F32)


def one_hot(mask):
    return jnp.where(mask, 1.0, 0.0).astype(BF)


def add_face(ref, tile, face, part):
    low = lax.broadcasted_iota(jnp.int32, (8, 128), 0) < 4
    for c in range(5):
        rows = part[16 * c : 16 * c + 16]
        if face < 2:
            ids = pl.ds(48 * face, 16)
            ref[tile, c, ids, :] = ref[tile, c, ids, :] + rows
        elif face >= 4:
            ids = pl.ds(3 * (face - 4), 16, stride=4)
            ref[tile, c, ids, :] = ref[tile, c, ids, :] + rows
        else:
            for v in range(2):
                both = rows[8 * v : 8 * v + 8]
                turned = pltpu.roll(both, 4, 0)
                for k in range(2):
                    ids = pl.ds(32 * v + 16 * k + 8 * (face - 2), 8)
                    value = both if k == face - 2 else turned
                    mask = low if face == 2 else jnp.logical_not(low)
                    ref[tile, c, ids, :] = ref[tile, c, ids, :] + jnp.where(mask, value, 0.0)


def face_rows(ref, tile, c, face):
    if face < 2:
        return ref[tile, c, 48 * face : 48 * face + 16, :]
    if face >= 4:
        return ref[tile, c, pl.ds(3 * (face - 4), 16, stride=4), :]
    low = lax.broadcasted_iota(jnp.int32, (8, 128), 0) < 4
    out = []
    for v in range(2):
        first = ref[tile, c, 32 * v + 8 * (face - 2) : 32 * v + 8 * (face - 2) + 8, :]
        second = ref[tile, c, 32 * v + 16 + 8 * (face - 2) : 32 * v + 24 + 8 * (face - 2), :]
        if face == 2:
            out.append(jnp.where(low, first, pltpu.roll(second, 4, 0)))
        else:
            out.append(jnp.where(low, pltpu.roll(first, 4, 0), second))
    return jnp.concatenate(out, axis=0)


def exchange(sectors, slabs, owned, *refs):
    hbm_refs = refs[:INPUTS]
    acc_ref, recv_ref, oh_ref, grad_ref = refs[INPUTS : INPUTS + 4]
    x_ref = refs[INPUTS + 4]
    vmem_refs = (None,) + refs[INPUTS + 5 : 2 * INPUTS + 4]
    (
        _,
        vel_ref,
        drag_ref,
        bw_ref,
        jac_ref,
        own_ref,
        nbrmat_ref,
        nbr_ref,
        sslots_ref,
        aslots_ref,
        live_ref,
        eb_ref,
        mats_ref,
    ) = vmem_refs
    (
        xs_ref,
        tr_ref,
        send_ref,
        a_ref,
        b_ref,
        bsend_ref,
        brecv_ref,
        send_sem,
        recv_sem,
        load_sem,
        x_sem,
    ) = refs[2 * INPUTS + 4 :]
    tiles = x_ref.shape[0]
    elems = tiles * 128
    slots = sslots_ref.shape[1]
    width = bsend_ref.shape[2]
    count = sectors * slabs

    loads = {
        k: pltpu.make_async_copy(hbm_refs[k], vmem_refs[k], load_sem.at[k])
        for k in range(1, INPUTS)
    }
    fields = {
        (t, h): pltpu.make_async_copy(
            hbm_refs[0].at[h, :, pl.ds(128 * t, 128)], x_ref.at[t, h], x_sem.at[5 * t + h]
        )
        for t in range(tiles)
        for h in range(5)
    }
    for k in (8, 9, 10, 6):
        loads[k].start()
    for key in fields:
        fields[key].start()
    for k in (1, 2, 3, 11, 12, 4, 5, 7):
        loads[k].start()

    sec = lax.axis_index("sector")
    axi = lax.axis_index("axial")
    joint = sec * slabs + axi
    prev = lax.rem(joint + count - 1, count)
    nxt = lax.rem(joint + 1, count)
    dev_prev = (prev // slabs, lax.rem(prev, slabs))
    dev_next = (nxt // slabs, lax.rem(nxt, slabs))
    dev_low = (lax.rem(sec + sectors - 1, sectors), axi)
    dev_high = (lax.rem(sec + 1, sectors), axi)

    barrier = pltpu.get_barrier_semaphore()
    for device in (dev_prev, dev_next, dev_low, dev_high):
        pl.semaphore_signal(barrier, inc=1, device_id=device, device_id_type=MESH)

    for k in (8, 9, 10, 6):
        loads[k].wait()
    slot_ids = lax.broadcasted_iota(jnp.int32, (1, slots), 1)
    rows_slots = lax.broadcasted_iota(jnp.int32, (elems, slots), 0)
    for i in range(4):
        row = i % 2
        ids = (sslots_ref if i < 2 else aslots_ref)[row : row + 1, :]
        if i < 2:
            ids = jnp.where(slot_ids < live_ref[:, row : row + 1], ids, -1)
        oh_ref[i] = one_hot(rows_slots == ids)

    lane = lax.broadcasted_iota(jnp.int32, (6, 256), 1)
    field = lane % 80 // 16
    diagonal = lax.broadcasted_iota(jnp.int32, (16, 256), 1)
    diagonal = diagonal % 16 == lax.broadcasted_iota(jnp.int32, (16, 256), 0)
    for c in range(5):
        value = jnp.where(field == 0, nbrmat_ref[c][:, 0:1], 0.0)
        for h in range(1, 5):
            value = jnp.where(field == h, nbrmat_ref[c][:, h : h + 1], value)
        value = 0.1 * value
        hi = value.astype(BF).astype(F32)
        value = jnp.where(lane < 160, hi, value - hi)
        for f in range(6):
            b_ref[f, 16 * c : 16 * c + 16, :] = jnp.where(
                diagonal, value[f : f + 1, :], 0.0
            ).astype(BF)

    def take_trace(t, face):
        lanes = slice(128 * t, 128 * t + 128)
        for c in range(5):
            hi, lo = split2(face_rows(x_ref, t, c, face))
            tr_ref[face, 16 * c : 16 * c + 16, lanes] = hi
            tr_ref[face, 80 + 16 * c : 96 + 16 * c, lanes] = lo

    for t in range(tiles):
        for h in range(5):
            fields[t, h].wait()
        for face in SIDES:
            take_trace(t, face)

    def through(face, both):
        hi, lo = both[:80].astype(BF), both[80:].astype(BF)
        return dot(b_ref[face, :, 0:240], jnp.concatenate([hi, lo, hi], axis=0))

    for i, face in enumerate(SIDES):
        send_ref[i] = through(face + 1 - 2 * (face % 2), dot(tr_ref[face], oh_ref[i]))

    pl.semaphore_wait(barrier, 4)

    def remote(src, dst, k, device):
        return pltpu.make_async_remote_copy(
            src_ref=src,
            dst_ref=dst,
            send_sem=send_sem.at[k],
            recv_sem=recv_sem.at[k],
            device_id=device,
            device_id_type=MESH,
        )

    up_x = remote(send_ref.at[1], recv_ref.at[0], 0, dev_high)
    down_x = remote(send_ref.at[0], recv_ref.at[1], 1, dev_low)
    up_z = remote(send_ref.at[3], recv_ref.at[2], 2, dev_next)
    down_z = remote(send_ref.at[2], recv_ref.at[3], 3, dev_prev)
    up_b = remote(bsend_ref.at[2], brecv_ref.at[0], 4, dev_next)
    down_b = remote(bsend_ref.at[0], brecv_ref.at[1], 5, dev_prev)
    has_low = axi > 0
    has_high = axi < slabs - 1
    up_x.start()
    down_x.start()

    @pl.when(has_high)
    def _():
        up_z.start()

    @pl.when(has_low)
    def _():
        down_z.start()

    @pl.when(jnp.logical_not(has_low))
    def _():
        recv_ref[2] = jnp.zeros((80, slots), F32)

    @pl.when(jnp.logical_not(has_high))
    def _():
        recv_ref[3] = jnp.zeros((80, slots), F32)

    for k in (1, 2, 3, 11, 12):
        loads[k].wait()
    parts = []
    for t in range(tiles):
        lanes = slice(128 * t, 128 * t + 128)
        total = x_ref[t, 1] * vel_ref[0, :, lanes].astype(F32)
        total += x_ref[t, 2] * vel_ref[1, :, lanes].astype(F32)
        total += x_ref[t, 3] * vel_ref[2, :, lanes].astype(F32)
        parts.append(jnp.sum(total * mats_ref[9], axis=0, keepdims=True))
    elem_grad = drag_ref[...] * jnp.concatenate(parts, axis=1)
    weighted = bw_ref[...] * elem_grad
    w1 = weighted.astype(BF)
    rest = weighted - w1.astype(F32)
    w2 = rest.astype(BF)
    w3 = (rest - w2.astype(F32)).astype(BF).astype(F32)
    row16 = lax.broadcasted_iota(jnp.int32, (16, elems), 0)
    stack = jnp.where(row16 == 0, w1.astype(F32), 0.0)
    stack = jnp.where(row16 == 1, w2.astype(F32), stack)
    stack = jnp.where(row16 == 2, w3, stack).astype(BF)
    rel = eb_ref[...] - (joint - 1) * owned
    rel = jnp.where(rel < 0, rel + BLOCKS, rel)
    rel = jnp.where(rel >= BLOCKS, rel - BLOCKS, rel)
    rows_blk = lax.broadcasted_iota(jnp.int32, (width, elems), 0)
    for j in range(3):
        sums = dot_nt(stack, one_hot(rows_blk == rel - j * owned))
        total = jnp.sum(sums, axis=0, keepdims=True)
        bsend_ref[j] = jnp.broadcast_to(total, (8, width))
    up_b.start()
    down_b.start()

    for k in (4, 5):
        loads[k].wait()
    spread = jnp.minimum(lax.broadcasted_iota(jnp.int32, (5, 384), 1) // 64, 4)
    spread = jnp.where(spread == lax.broadcasted_iota(jnp.int32, (5, 384), 0), 1.0, 0.0)
    for c in range(5):
        rows = slice(64 * c, 64 * c + 64)
        jac = jac_ref[0][:, c : c + 1] * spread[0:1, :]
        face = own_ref[c][:, 0:1] * spread[0:1, :]
        for h in range(1, 5):
            jac += jac_ref[h][:, c : c + 1] * spread[h : h + 1, :]
            face += own_ref[c][:, h : h + 1] * spread[h : h + 1, :]
        for t in range(3):
            lanes = slice(128 * t, 128 * t + 128)
            total = mats_ref[0] * jac[0:1, lanes]
            for j in range(1, 9):
                row = jac[j : j + 1, lanes] if j < 3 else face[j - 3 : j - 2, lanes]
                total += mats_ref[j] * row
            hi, lo = split2(total)
            places = ((768, hi), (896, lo)) if t == 2 else ((0, hi), (256, hi), (512, lo))
            for base, part in places:
                base += 128 * t if t < 2 else 0
                a_ref[rows, base : base + 128] = part

    for t in range(tiles):
        lanes = slice(128 * t, 128 * t + 128)
        for h in range(5):
            hi, lo = split2(x_ref[t, h])
            places = ((768, hi), (832, lo), (896, hi))
            if h < 4:
                places = ((64 * h, hi), (256 + 64 * h, lo), (512 + 64 * h, hi))
            for base, part in places:
                xs_ref[base : base + 64, lanes] = part
        for face in (2, 3):
            take_trace(t, face)

    own = dot(a_ref[:, 0:960], xs_ref[...])
    keep = 1.0 - 0.1 * drag_ref[...]
    for t in range(tiles):
        lanes = slice(128 * t, 128 * t + 128)
        for c in range(5):
            x = x_ref[t, c]
            scaled = x * keep[:, lanes] if 1 <= c <= 3 else x
            acc_ref[t, c] = scaled + own[64 * c : 64 * c + 64, lanes]

    loads[7].wait()
    chunk = 256
    rows_src = lax.broadcasted_iota(jnp.int32, (chunk, elems), 0)
    for f in range(6):
        ids = nbr_ref[f : f + 1, :]
        g = f + 1 - 2 * (f % 2)
        both = jnp.zeros((160, elems), F32)
        for k in range(elems // chunk):
            hot = one_hot(rows_src == ids - k * chunk)
            both += dot(tr_ref[g, :, k * chunk : (k + 1) * chunk], hot)
        part = through(f, both)
        for t in range(tiles):
            add_face(acc_ref, t, f, part[:, 128 * t : 128 * t + 128])

    up_b.wait()
    down_b.wait()
    grad_ref[...] = bsend_ref[1] + brecv_ref[0] + brecv_ref[1]

    up_x.wait()
    down_x.wait()

    @pl.when(has_high)
    def _():
        up_z.wait_send()
        down_z.wait_recv()

    @pl.when(has_low)
    def _():
        down_z.wait_send()
        up_z.wait_recv()


def finish(acc_ref, recv_ref, oh_ref, sums_ref, out_ref, grad_ref, o_ref, g_ref, sem):
    tiles = acc_ref.shape[0]
    g_ref[...] = sums_ref[0, : g_ref.shape[0]]
    grad_copy = pltpu.make_async_copy(g_ref, grad_ref, sem.at[tiles])
    grad_copy.start()
    copies = []
    halves = [jnp.concatenate(split2(recv_ref[i]), axis=0) for i in range(4)]
    for first in range(0, tiles, 2):
        for t in (first, first + 1):
            o_ref[t] = acc_ref[t]
        for i, face in enumerate(SIDES):
            both = dot_nt(halves[i], oh_ref[i, 128 * first : 128 * first + 256, :])
            part = both[:80] + both[80:]
            for k in range(2):
                add_face(o_ref, first + k, face, part[:, 128 * k : 128 * k + 128])
        for t in (first, first + 1):
            copy = pltpu.make_async_copy(
                o_ref.at[t], out_ref.at[:, :, pl.ds(128 * t, 128)], sem.at[t]
            )
            copy.start()
            copies.append(copy)
    for copy in copies:
        copy.wait()
    grad_copy.wait()


def on_device(
    sectors,
    slabs,
    adjoint,
    velocity,
    drag,
    block_weight,
    flux_jac,
    face_own,
    face_nbr,
    nbr_local,
    sector_slots,
    axial_slots,
    sector_live,
    elem_block,
):
    elems = adjoint.shape[2]
    tiles = elems // 128
    slots = sector_slots.shape[1]
    owned = BLOCKS // (sectors * slabs)
    width = -(-owned // 128) * 128
    operands = (
        adjoint,
        velocity,
        drag.reshape(1, elems),
        block_weight.reshape(1, elems),
        jnp.transpose(flux_jac, (1, 0, 2)),
        jnp.transpose(face_own, (1, 0, 2)),
        jnp.transpose(face_nbr, (1, 0, 2)),
        nbr_local,
        sector_slots,
        axial_slots,
        sector_live.reshape(1, 2),
        elem_block.reshape(1, elems),
        constant_tables(),
    )
    vmem = pl.BlockSpec(memory_space=pltpu.VMEM)
    hbm = pl.BlockSpec(memory_space=pltpu.HBM)
    handed = pl.pallas_call(
        functools.partial(exchange, sectors, slabs, owned),
        out_shape=(
            pltpu.VMEM((tiles, 5, 64, 128), F32),
            pltpu.VMEM((4, 80, slots), F32),
            pltpu.VMEM((4, elems, slots), BF),
            pltpu.VMEM((8, width), F32),
        ),
        in_specs=[hbm] * INPUTS,
        out_specs=(vmem,) * 4,
        scratch_shapes=[pltpu.VMEM((tiles, 5, 64, 128), F32)]
        + [pltpu.VMEM(a.shape, a.dtype) for a in operands[1:]]
        + [
            pltpu.VMEM((960, elems), BF),
            pltpu.VMEM((6, 160, elems), BF),
            pltpu.VMEM((4, 80, slots), F32),
            pltpu.VMEM((320, 1024), BF),
            pltpu.VMEM((6, 80, 256), BF),
            pltpu.VMEM((3, 8, width), F32),
            pltpu.VMEM((2, 8, width), F32),
            pltpu.SemaphoreType.DMA((6,)),
            pltpu.SemaphoreType.DMA((6,)),
            pltpu.SemaphoreType.DMA((INPUTS,)),
            pltpu.SemaphoreType.DMA((5 * tiles,)),
        ],
        compiler_params=pltpu.CompilerParams(
            collective_id=0, has_side_effects=True, vmem_limit_bytes=60 * 1024 * 1024
        ),
    )(*operands)
    return pl.pallas_call(
        finish,
        out_shape=(
            jax.ShapeDtypeStruct(adjoint.shape, F32),
            jax.ShapeDtypeStruct((owned,), F32),
        ),
        in_specs=[vmem] * 4,
        out_specs=(hbm, hbm),
        scratch_shapes=[
            pltpu.VMEM((tiles, 5, 64, 128), F32),
            pltpu.VMEM((owned,), F32),
            pltpu.SemaphoreType.DMA((tiles + 1,)),
        ],
        compiler_params=pltpu.CompilerParams(vmem_limit_bytes=40 * 1024 * 1024),
    )(*handed)


def solution(mesh):
    placed = (
        P(None, None, ("sector", "axial")),
        P(None, None, ("sector", "axial")),
        P(("sector", "axial")),
        P(("sector", "axial")),
        P(),
        P(),
        P(),
        P(None, ("sector", "axial")),
        P(None, ("sector", "axial")),
        P(None, ("sector", "axial")),
        P("sector", "axial", None),
        P(("sector", "axial")),
    )
    return jax.shard_map(
        functools.partial(on_device, mesh.shape["sector"], mesh.shape["axial"]),
        mesh=mesh,
        in_specs=placed,
        out_specs=(P(None, None, ("sector", "axial")), P(("sector", "axial"))),
        check_vma=False,
    )
```

time: 15.9 us -> 17 us (1.069)
  Pallas kernels: 13.5 us -> 16.2 us
  local copies, waits for them, and re-layouts: 1.57 us -> 0 us
    pallas_call x1 -> x2, Pallas kernels: 13.5 us -> 16.2 us  [the longest x1 14.5 us: on_device(): pl.pallas_call(functools.partial(exchange, sectors, slabs, owned), out_sh...]
    unnamed x2 -> x0, local copies, waits for them, and re-layouts: 1.57 us -> none
where the time goes in v1:
time: 17 us; the launch traced here: 16.8 us
  Pallas kernels  16.2 us (95%)
  between operations  0.64 us (4%)
    pallas_call x1, Pallas kernels, on_device(): pl.pallas_call(functools.partial(exchange, sectors, slabs, owned), out_sh...  14.5 us
    pallas_call x1, Pallas kernels, on_device(): pl.pallas_call(finish, out_shape=(jax.ShapeDtypeStruct(adjoint.shape, F32...  1.66 us

profile of v1, /device:TPU:0, one launch (start us, length us, event | category | flops | bytes accessed | tf_op | source)
XLA Modules:
  0.0 16.8 jit_solution(14190541538151500721)
XLA Ops:
  0.6 14.5 %shard_map.140 = (f32[8,5,64,128]{3,2,1,0:T(8,128)S(1)}, f32[4,80,256]{2,1,0:T(8,128)S(1)}, bf16[4,1024,256]{2,1,0:T(8,128)(2,1)S(1)}, f32[8,128]{1,0:T(8,128)S(1)}) custom-call(f32[5,64,1024]{2,1,0:T(8,128)} %refs_0_.1, bf16[3,64,1024]{2,1,0:T(8,128)(2,1)} %refs_1_.1, f32[1,1024]{1,0:T(1,128)} %bitcast.10, f32[1,1024]{1,0:T(1,128)} %bitcast.11, ...), custom_call_target="tpu_custom_call" | custom-call | tf_op jit(solution)/shard_map/pallas_call | solution.py:440
  15.1 1.7 %shard_map.141 = (f32[5,64,1024]{2,1,0:T(8,128)}, f32[128]{0:T(128)}) custom-call(f32[8,5,64,128]{3,2,1,0:T(8,128)S(1)} %get-tuple-element.6.acc_ref, f32[4,80,256]{2,1,0:T(8,128)S(1)} %get-tuple-element.7.recv_ref, bf16[4,1024,256]{2,1,0:T(8,128)(2,1)S(1)} %get-tuple-element.8.oh_ref, f32[8,128]{1,0:T(8,128)S(1)} %get-tuple-element.9.sums_ref), custom_call_target="tpu_custom_call" | custom-call | tf_op jit(solution)/shard_map/pallas_call | solution.py:469

commit v2 on v1

--- a/solution.py
+++ b/solution.py
@@ -69,13 +69,13 @@
 
 
 def one_hot(mask):
-    return jnp.where(mask, 1.0, 0.0).astype(BF)
+    return jnp.where(mask, jnp.ones((), BF), jnp.zeros((), BF))
 
 
 def add_face(ref, tile, face, part):
     low = lax.broadcasted_iota(jnp.int32, (8, 128), 0) < 4
     for c in range(5):
-        rows = part[16 * c : 16 * c + 16]
+        rows = part[c]
         if face < 2:
             ids = pl.ds(48 * face, 16)
             ref[tile, c, ids, :] = ref[tile, c, ids, :] + rows
@@ -91,6 +91,13 @@
                     value = both if k == face - 2 else turned
                     mask = low if face == 2 else jnp.logical_not(low)
                     ref[tile, c, ids, :] = ref[tile, c, ids, :] + jnp.where(mask, value, 0.0)
+
+
+def mixed(coef_ref, face, c, parts):
+    total = coef_ref[5 * c, face : face + 1, :] * parts[0]
+    for h in range(1, 5):
+        total += coef_ref[5 * c + h, face : face + 1, :] * parts[h]
+    return total
 
 
 def face_rows(ref, tile, c, face):
@@ -135,7 +142,7 @@
         tr_ref,
         send_ref,
         a_ref,
-        b_ref,
+        coef_ref,
         bsend_ref,
         brecv_ref,
         send_sem,
@@ -184,29 +191,18 @@
     for k in (8, 9, 10, 6):
         loads[k].wait()
     slot_ids = lax.broadcasted_iota(jnp.int32, (1, slots), 1)
-    rows_slots = lax.broadcasted_iota(jnp.int32, (elems, slots), 0)
+    rows_slots = lax.broadcasted_iota(jnp.int32, (elems, slots), 0).astype(jnp.int16)
     for i in range(4):
         row = i % 2
         ids = (sslots_ref if i < 2 else aslots_ref)[row : row + 1, :]
         if i < 2:
             ids = jnp.where(slot_ids < live_ref[:, row : row + 1], ids, -1)
+        ids = jnp.broadcast_to(ids, (elems, slots)).astype(jnp.int16)
         oh_ref[i] = one_hot(rows_slots == ids)
 
-    lane = lax.broadcasted_iota(jnp.int32, (6, 256), 1)
-    field = lane % 80 // 16
-    diagonal = lax.broadcasted_iota(jnp.int32, (16, 256), 1)
-    diagonal = diagonal % 16 == lax.broadcasted_iota(jnp.int32, (16, 256), 0)
     for c in range(5):
-        value = jnp.where(field == 0, nbrmat_ref[c][:, 0:1], 0.0)
-        for h in range(1, 5):
-            value = jnp.where(field == h, nbrmat_ref[c][:, h : h + 1], value)
-        value = 0.1 * value
-        hi = value.astype(BF).astype(F32)
-        value = jnp.where(lane < 160, hi, value - hi)
-        for f in range(6):
-            b_ref[f, 16 * c : 16 * c + 16, :] = jnp.where(
-                diagonal, value[f : f + 1, :], 0.0
-            ).astype(BF)
+        for h in range(5):
+            coef_ref[5 * c + h] = jnp.broadcast_to(0.1 * nbrmat_ref[c][:, h : h + 1], (6, 128))
 
     def take_trace(t, face):
         lanes = slice(128 * t, 128 * t + 128)
@@ -215,18 +211,20 @@
             tr_ref[face, 16 * c : 16 * c + 16, lanes] = hi
             tr_ref[face, 80 + 16 * c : 96 + 16 * c, lanes] = lo
 
+    for key in fields:
+        fields[key].wait()
     for t in range(tiles):
-        for h in range(5):
-            fields[t, h].wait()
         for face in SIDES:
             take_trace(t, face)
 
-    def through(face, both):
-        hi, lo = both[:80].astype(BF), both[80:].astype(BF)
-        return dot(b_ref[face, :, 0:240], jnp.concatenate([hi, lo, hi], axis=0))
-
     for i, face in enumerate(SIDES):
-        send_ref[i] = through(face + 1 - 2 * (face % 2), dot(tr_ref[face], oh_ref[i]))
+        both = dot(tr_ref[face], oh_ref[i])
+        both = both[:80] + both[80:]
+        for n in range(0, slots, 128):
+            parts = [both[16 * h : 16 * h + 16, n : n + 128] for h in range(5)]
+            for c in range(5):
+                value = mixed(coef_ref, face + 1 - 2 * (face % 2), c, parts)
+                send_ref[i, 16 * c : 16 * c + 16, n : n + 128] = value
 
     pl.semaphore_wait(barrier, 4)
 
@@ -289,9 +287,10 @@
     rel = eb_ref[...] - (joint - 1) * owned
     rel = jnp.where(rel < 0, rel + BLOCKS, rel)
     rel = jnp.where(rel >= BLOCKS, rel - BLOCKS, rel)
-    rows_blk = lax.broadcasted_iota(jnp.int32, (width, elems), 0)
+    rows_blk = lax.broadcasted_iota(jnp.int32, (width, elems), 0).astype(jnp.int16)
     for j in range(3):
-        sums = dot_nt(stack, one_hot(rows_blk == rel - j * owned))
+        ids = jnp.broadcast_to(rel - j * owned, (width, elems)).astype(jnp.int16)
+        sums = dot_nt(stack, one_hot(rows_blk == ids))
         total = jnp.sum(sums, axis=0, keepdims=True)
         bsend_ref[j] = jnp.broadcast_to(total, (8, width))
     up_b.start()
@@ -342,18 +341,15 @@
             acc_ref[t, c] = scaled + own[64 * c : 64 * c + 64, lanes]
 
     loads[7].wait()
-    chunk = 256
-    rows_src = lax.broadcasted_iota(jnp.int32, (chunk, elems), 0)
+    rows_src = lax.broadcasted_iota(jnp.int32, (elems, elems), 0).astype(jnp.int16)
     for f in range(6):
-        ids = nbr_ref[f : f + 1, :]
         g = f + 1 - 2 * (f % 2)
-        both = jnp.zeros((160, elems), F32)
-        for k in range(elems // chunk):
-            hot = one_hot(rows_src == ids - k * chunk)
-            both += dot(tr_ref[g, :, k * chunk : (k + 1) * chunk], hot)
-        part = through(f, both)
+        ids = jnp.broadcast_to(nbr_ref[f : f + 1, :], (elems, elems)).astype(jnp.int16)
+        both = dot(tr_ref[g], one_hot(rows_src == ids))
+        both = both[:80] + both[80:]
         for t in range(tiles):
-            add_face(acc_ref, t, f, part[:, 128 * t : 128 * t + 128])
+            parts = [both[16 * h : 16 * h + 16, 128 * t : 128 * t + 128] for h in range(5)]
+            add_face(acc_ref, t, f, [mixed(coef_ref, f, c, parts) for c in range(5)])
 
     up_b.wait()
     down_b.wait()
@@ -387,7 +383,9 @@
             both = dot_nt(halves[i], oh_ref[i, 128 * first : 128 * first + 256, :])
             part = both[:80] + both[80:]
             for k in range(2):
-                add_face(o_ref, first + k, face, part[:, 128 * k : 128 * k + 128])
+                lanes = slice(128 * k, 128 * k + 128)
+                rows = [part[16 * c : 16 * c + 16, lanes] for c in range(5)]
+                add_face(o_ref, first + k, face, rows)
         for t in (first, first + 1):
             copy = pltpu.make_async_copy(
                 o_ref.at[t], out_ref.at[:, :, pl.ds(128 * t, 128)], sem.at[t]
@@ -454,7 +452,7 @@
             pltpu.VMEM((6, 160, elems), BF),
             pltpu.VMEM((4, 80, slots), F32),
             pltpu.VMEM((320, 1024), BF),
-            pltpu.VMEM((6, 80, 256), BF),
+            pltpu.VMEM((25, 6, 128), F32),
             pltpu.VMEM((3, 8, width), F32),
             pltpu.VMEM((2, 8, width), F32),
             pltpu.SemaphoreType.DMA((6,)),

time: 17 us -> 14.7 us (0.86)
  Pallas kernels: 16.2 us -> 13.9 us
    pallas_call x1, Pallas kernels: 14.5 us -> 12.2 us  [on_device(): pl.pallas_call(functools.partial(exchange, sectors, slabs, owned), out_sh...]
where the time goes in v2:
time: 14.7 us; the launch traced here: 14.5 us
  Pallas kernels  13.9 us (95%)
  between operations  0.64 us (4%)
    pallas_call x1, Pallas kernels, on_device(): pl.pallas_call(functools.partial(exchange, sectors, slabs, owned), out_sh...  12.2 us
    pallas_call x1, Pallas kernels, on_device(): pl.pallas_call(finish, out_shape=(jax.ShapeDtypeStruct(adjoint.shape, F32...  1.66 us

profile of v2, /device:TPU:0, one launch (start us, length us, event | category | flops | bytes accessed | tf_op | source)
XLA Modules:
  0.0 14.5 jit_solution(10623870589296885884)
XLA Ops:
  0.6 12.2 %shard_map.140 = (f32[8,5,64,128]{3,2,1,0:T(8,128)S(1)}, f32[4,80,256]{2,1,0:T(8,128)S(1)}, bf16[4,1024,256]{2,1,0:T(8,128)(2,1)S(1)}, f32[8,128]{1,0:T(8,128)S(1)}) custom-call(f32[5,64,1024]{2,1,0:T(8,128)} %refs_0_.1, bf16[3,64,1024]{2,1,0:T(8,128)(2,1)} %refs_1_.1, f32[1,1024]{1,0:T(1,128)} %bitcast.10, f32[1,1024]{1,0:T(1,128)} %bitcast.11, ...), custom_call_target="tpu_custom_call" | custom-call | tf_op jit(solution)/shard_map/pallas_call | solution.py:438
  12.9 1.7 %shard_map.141 = (f32[5,64,1024]{2,1,0:T(8,128)}, f32[128]{0:T(128)}) custom-call(f32[8,5,64,128]{3,2,1,0:T(8,128)S(1)} %get-tuple-element.6.acc_ref, f32[4,80,256]{2,1,0:T(8,128)S(1)} %get-tuple-element.7.recv_ref, bf16[4,1024,256]{2,1,0:T(8,128)(2,1)S(1)} %get-tuple-element.8.oh_ref, f32[8,128]{1,0:T(8,128)S(1)} %get-tuple-element.9.sums_ref), custom_call_target="tpu_custom_call" | custom-call | tf_op jit(solution)/shard_map/pallas_call | solution.py:467

commit v3 on v2

--- a/solution.py
+++ b/solution.py
@@ -12,7 +12,7 @@
 BF = jnp.bfloat16
 F32 = jnp.float32
 MESH = pl.DeviceIdType.MESH
-INPUTS = 13
+INPUTS = 14
 SIDES = (0, 1, 4, 5)
 
 
@@ -51,8 +51,8 @@
         diag[ids.reshape(16), ids.reshape(16)] = 1.0
         mats.append(diag)
     mats = [0.1 * np.concatenate([m, m], axis=1) for m in mats]
-    mats.append(np.repeat(node_weight[:, None], 128, axis=1))
-    return jnp.asarray(np.stack(mats), F32)
+    weights = np.repeat(node_weight[:, None], 128, axis=1)
+    return jnp.asarray(np.stack(mats), F32), jnp.asarray(weights, F32)
 
 
 def split2(x):
@@ -119,9 +119,9 @@
 
 def exchange(sectors, slabs, owned, *refs):
     hbm_refs = refs[:INPUTS]
-    acc_ref, recv_ref, oh_ref, grad_ref = refs[INPUTS : INPUTS + 4]
-    x_ref = refs[INPUTS + 4]
-    vmem_refs = (None,) + refs[INPUTS + 5 : 2 * INPUTS + 4]
+    acc_ref, grad_ref = refs[INPUTS : INPUTS + 2]
+    x_ref = refs[INPUTS + 2]
+    vmem_refs = (None,) + refs[INPUTS + 3 : 2 * INPUTS + 2]
     (
         _,
         vel_ref,
@@ -136,20 +136,24 @@
         live_ref,
         eb_ref,
         mats_ref,
+        weight_ref,
     ) = vmem_refs
     (
         xs_ref,
         tr_ref,
+        oh_ref,
         send_ref,
+        recv_ref,
         a_ref,
         coef_ref,
         bsend_ref,
         brecv_ref,
         send_sem,
         recv_sem,
+        far_sem,
         load_sem,
         x_sem,
-    ) = refs[2 * INPUTS + 4 :]
+    ) = refs[2 * INPUTS + 2 :]
     tiles = x_ref.shape[0]
     elems = tiles * 128
     slots = sslots_ref.shape[1]
@@ -164,14 +168,14 @@
         (t, h): pltpu.make_async_copy(
             hbm_refs[0].at[h, :, pl.ds(128 * t, 128)], x_ref.at[t, h], x_sem.at[5 * t + h]
         )
+        for h in (1, 2, 3, 0, 4)
         for t in range(tiles)
-        for h in range(5)
     }
-    for k in (8, 9, 10, 6):
+    for k in (1, 13, 2, 3, 11):
         loads[k].start()
     for key in fields:
         fields[key].start()
-    for k in (1, 2, 3, 11, 12, 4, 5, 7):
+    for k in (8, 9, 10, 6, 7, 12, 4, 5):
         loads[k].start()
 
     sec = lax.axis_index("sector")
@@ -184,96 +188,37 @@
     dev_low = (lax.rem(sec + sectors - 1, sectors), axi)
     dev_high = (lax.rem(sec + 1, sectors), axi)
 
-    barrier = pltpu.get_barrier_semaphore()
-    for device in (dev_prev, dev_next, dev_low, dev_high):
-        pl.semaphore_signal(barrier, inc=1, device_id=device, device_id_type=MESH)
-
-    for k in (8, 9, 10, 6):
-        loads[k].wait()
-    slot_ids = lax.broadcasted_iota(jnp.int32, (1, slots), 1)
-    rows_slots = lax.broadcasted_iota(jnp.int32, (elems, slots), 0).astype(jnp.int16)
-    for i in range(4):
-        row = i % 2
-        ids = (sslots_ref if i < 2 else aslots_ref)[row : row + 1, :]
-        if i < 2:
-            ids = jnp.where(slot_ids < live_ref[:, row : row + 1], ids, -1)
-        ids = jnp.broadcast_to(ids, (elems, slots)).astype(jnp.int16)
-        oh_ref[i] = one_hot(rows_slots == ids)
-
-    for c in range(5):
-        for h in range(5):
-            coef_ref[5 * c + h] = jnp.broadcast_to(0.1 * nbrmat_ref[c][:, h : h + 1], (6, 128))
-
-    def take_trace(t, face):
-        lanes = slice(128 * t, 128 * t + 128)
-        for c in range(5):
-            hi, lo = split2(face_rows(x_ref, t, c, face))
-            tr_ref[face, 16 * c : 16 * c + 16, lanes] = hi
-            tr_ref[face, 80 + 16 * c : 96 + 16 * c, lanes] = lo
-
-    for key in fields:
-        fields[key].wait()
-    for t in range(tiles):
-        for face in SIDES:
-            take_trace(t, face)
-
-    for i, face in enumerate(SIDES):
-        both = dot(tr_ref[face], oh_ref[i])
-        both = both[:80] + both[80:]
-        for n in range(0, slots, 128):
-            parts = [both[16 * h : 16 * h + 16, n : n + 128] for h in range(5)]
-            for c in range(5):
-                value = mixed(coef_ref, face + 1 - 2 * (face % 2), c, parts)
-                send_ref[i, 16 * c : 16 * c + 16, n : n + 128] = value
-
-    pl.semaphore_wait(barrier, 4)
-
-    def remote(src, dst, k, device):
-        return pltpu.make_async_remote_copy(
-            src_ref=src,
-            dst_ref=dst,
-            send_sem=send_sem.at[k],
-            recv_sem=recv_sem.at[k],
-            device_id=device,
-            device_id_type=MESH,
-        )
-
-    up_x = remote(send_ref.at[1], recv_ref.at[0], 0, dev_high)
-    down_x = remote(send_ref.at[0], recv_ref.at[1], 1, dev_low)
-    up_z = remote(send_ref.at[3], recv_ref.at[2], 2, dev_next)
-    down_z = remote(send_ref.at[2], recv_ref.at[3], 3, dev_prev)
-    up_b = remote(bsend_ref.at[2], brecv_ref.at[0], 4, dev_next)
-    down_b = remote(bsend_ref.at[0], brecv_ref.at[1], 5, dev_prev)
     has_low = axi > 0
     has_high = axi < slabs - 1
-    up_x.start()
-    down_x.start()
+
+    barrier = pltpu.get_barrier_semaphore()
+
+    def greet(device):
+        pl.semaphore_signal(barrier, inc=1, device_id=device, device_id_type=MESH)
+
+    greet(dev_low)
+    greet(dev_high)
+
+    @pl.when(has_low)
+    def _():
+        greet(dev_prev)
 
     @pl.when(has_high)
     def _():
-        up_z.start()
-
-    @pl.when(has_low)
-    def _():
-        down_z.start()
-
-    @pl.when(jnp.logical_not(has_low))
-    def _():
-        recv_ref[2] = jnp.zeros((80, slots), F32)
-
-    @pl.when(jnp.logical_not(has_high))
-    def _():
-        recv_ref[3] = jnp.zeros((80, slots), F32)
-
-    for k in (1, 2, 3, 11, 12):
+        greet(dev_next)
+
+    for k in (1, 13, 2, 3, 11):
         loads[k].wait()
+    for h in (1, 2, 3):
+        for t in range(tiles):
+            fields[t, h].wait()
     parts = []
     for t in range(tiles):
         lanes = slice(128 * t, 128 * t + 128)
         total = x_ref[t, 1] * vel_ref[0, :, lanes].astype(F32)
         total += x_ref[t, 2] * vel_ref[1, :, lanes].astype(F32)
         total += x_ref[t, 3] * vel_ref[2, :, lanes].astype(F32)
-        parts.append(jnp.sum(total * mats_ref[9], axis=0, keepdims=True))
+        parts.append(jnp.sum(total * weight_ref[...], axis=0, keepdims=True))
     elem_grad = drag_ref[...] * jnp.concatenate(parts, axis=1)
     weighted = bw_ref[...] * elem_grad
     w1 = weighted.astype(BF)
@@ -293,11 +238,99 @@
         sums = dot_nt(stack, one_hot(rows_blk == ids))
         total = jnp.sum(sums, axis=0, keepdims=True)
         bsend_ref[j] = jnp.broadcast_to(total, (8, width))
+    def remote(src, dst, k, device):
+        return pltpu.make_async_remote_copy(
+            src_ref=src,
+            dst_ref=dst,
+            send_sem=send_sem.at[k],
+            recv_sem=recv_sem.at[k],
+            device_id=device,
+            device_id_type=MESH,
+        )
+
+    up_x = remote(send_ref.at[1], recv_ref.at[0], 0, dev_high)
+    down_x = remote(send_ref.at[0], recv_ref.at[1], 1, dev_low)
+    up_z = remote(send_ref.at[3], recv_ref.at[2], 2, dev_next)
+    down_z = remote(send_ref.at[2], recv_ref.at[3], 3, dev_prev)
+    up_b = remote(bsend_ref.at[2], brecv_ref.at[0], 4, dev_next)
+    down_b = remote(bsend_ref.at[0], brecv_ref.at[1], 5, dev_prev)
+
+    @pl.when(has_low)
+    def _():
+        pl.semaphore_wait(barrier, 4)
+        down_b.start()
+
+    @pl.when(jnp.logical_not(has_low))
+    def _():
+        pl.semaphore_wait(barrier, 3)
+        greet(dev_prev)
+
+    @pl.when(jnp.logical_not(has_high))
+    def _():
+        pl.semaphore_signal(far_sem, inc=1, device_id=dev_next, device_id_type=MESH)
+
     up_b.start()
-    down_b.start()
-
-    for k in (4, 5):
+    for k in (8, 9, 10, 6):
         loads[k].wait()
+    slot_ids = lax.broadcasted_iota(jnp.int32, (1, slots), 1)
+    rows_slots = lax.broadcasted_iota(jnp.int32, (elems, slots), 0).astype(jnp.int16)
+    for i in range(4):
+        row = i % 2
+        ids = (sslots_ref if i < 2 else aslots_ref)[row : row + 1, :]
+        if i < 2:
+            ids = jnp.where(slot_ids < live_ref[:, row : row + 1], ids, -1)
+        ids = jnp.broadcast_to(ids, (elems, slots)).astype(jnp.int16)
+        oh_ref[i] = one_hot(rows_slots == ids)
+
+    for c in range(5):
+        for h in range(5):
+            coef_ref[5 * c + h] = jnp.broadcast_to(0.1 * nbrmat_ref[c][:, h : h + 1], (6, 128))
+
+    def take_trace(t, face):
+        lanes = slice(128 * t, 128 * t + 128)
+        for c in range(5):
+            hi, lo = split2(face_rows(x_ref, t, c, face))
+            tr_ref[face, 16 * c : 16 * c + 16, lanes] = hi
+            tr_ref[face, 80 + 16 * c : 96 + 16 * c, lanes] = lo
+
+    for h in (0, 4):
+        for t in range(tiles):
+            fields[t, h].wait()
+    for t in range(tiles):
+        for face in SIDES:
+            take_trace(t, face)
+
+    for i, face in enumerate(SIDES):
+        both = dot(tr_ref[face], oh_ref[i])
+        both = both[:80] + both[80:]
+        for n in range(0, slots, 128):
+            parts = [both[16 * h : 16 * h + 16, n : n + 128] for h in range(5)]
+            for c in range(5):
+                value = mixed(coef_ref, face + 1 - 2 * (face % 2), c, parts)
+                send_ref[i, 16 * c : 16 * c + 16, n : n + 128] = value
+
+    up_x.start()
+    down_x.start()
+
+    @pl.when(has_high)
+    def _():
+        up_z.start()
+
+    @pl.when(has_low)
+    def _():
+        down_z.start()
+
+    @pl.when(jnp.logical_not(has_low))
+    def _():
+        recv_ref[2] = jnp.zeros((80, slots), F32)
+
+    @pl.when(jnp.logical_not(has_high))
+    def _():
+        recv_ref[3] = jnp.zeros((80, slots), F32)
+
+    for k in (7, 12, 4, 5):
+        loads[k].wait()
+
     spread = jnp.minimum(lax.broadcasted_iota(jnp.int32, (5, 384), 1) // 64, 4)
     spread = jnp.where(spread == lax.broadcasted_iota(jnp.int32, (5, 384), 0), 1.0, 0.0)
     for c in range(5):
@@ -340,7 +373,6 @@
             scaled = x * keep[:, lanes] if 1 <= c <= 3 else x
             acc_ref[t, c] = scaled + own[64 * c : 64 * c + 64, lanes]
 
-    loads[7].wait()
     rows_src = lax.broadcasted_iota(jnp.int32, (elems, elems), 0).astype(jnp.int16)
     for f in range(6):
         g = f + 1 - 2 * (f % 2)
@@ -351,50 +383,47 @@
             parts = [both[16 * h : 16 * h + 16, 128 * t : 128 * t + 128] for h in range(5)]
             add_face(acc_ref, t, f, [mixed(coef_ref, f, c, parts) for c in range(5)])
 
+    @pl.when(jnp.logical_not(has_low))
+    def _():
+        pl.semaphore_wait(far_sem, 1)
+        down_b.start()
+
+    up_x.wait()
+    down_x.wait()
+
+    @pl.when(has_high)
+    def _():
+        up_z.wait_send()
+        down_z.wait_recv()
+
+    @pl.when(has_low)
+    def _():
+        down_z.wait_send()
+        up_z.wait_recv()
+
+    for i, face in enumerate(SIDES):
+        both = dot_nt(jnp.concatenate(split2(recv_ref[i]), axis=0), oh_ref[i])
+        both = both[:80] + both[80:]
+        for t in range(tiles):
+            lanes = slice(128 * t, 128 * t + 128)
+            add_face(acc_ref, t, face, [both[16 * c : 16 * c + 16, lanes] for c in range(5)])
+
     up_b.wait()
     down_b.wait()
-    grad_ref[...] = bsend_ref[1] + brecv_ref[0] + brecv_ref[1]
-
-    up_x.wait()
-    down_x.wait()
-
-    @pl.when(has_high)
-    def _():
-        up_z.wait_send()
-        down_z.wait_recv()
-
-    @pl.when(has_low)
-    def _():
-        down_z.wait_send()
-        up_z.wait_recv()
-
-
-def finish(acc_ref, recv_ref, oh_ref, sums_ref, out_ref, grad_ref, o_ref, g_ref, sem):
+    sums = bsend_ref[1] + brecv_ref[0] + brecv_ref[1]
+    grad_ref[...] = sums[0, :owned]
+
+
+def finish(acc_ref, sums_ref, out_ref, grad_ref, sem):
     tiles = acc_ref.shape[0]
-    g_ref[...] = sums_ref[0, : g_ref.shape[0]]
-    grad_copy = pltpu.make_async_copy(g_ref, grad_ref, sem.at[tiles])
-    grad_copy.start()
-    copies = []
-    halves = [jnp.concatenate(split2(recv_ref[i]), axis=0) for i in range(4)]
-    for first in range(0, tiles, 2):
-        for t in (first, first + 1):
-            o_ref[t] = acc_ref[t]
-        for i, face in enumerate(SIDES):
-            both = dot_nt(halves[i], oh_ref[i, 128 * first : 128 * first + 256, :])
-            part = both[:80] + both[80:]
-            for k in range(2):
-                lanes = slice(128 * k, 128 * k + 128)
-                rows = [part[16 * c : 16 * c + 16, lanes] for c in range(5)]
-                add_face(o_ref, first + k, face, rows)
-        for t in (first, first + 1):
-            copy = pltpu.make_async_copy(
-                o_ref.at[t], out_ref.at[:, :, pl.ds(128 * t, 128)], sem.at[t]
-            )
-            copy.start()
-            copies.append(copy)
+    copies = [pltpu.make_async_copy(sums_ref, grad_ref, sem.at[tiles])]
+    for t in range(tiles):
+        place = out_ref.at[:, :, pl.ds(128 * t, 128)]
+        copies.append(pltpu.make_async_copy(acc_ref.at[t], place, sem.at[t]))
+    for copy in copies:
+        copy.start()
     for copy in copies:
         copy.wait()
-    grad_copy.wait()
 
 
 def on_device(
@@ -431,7 +460,7 @@
         axial_slots,
         sector_live.reshape(1, 2),
         elem_block.reshape(1, elems),
-        constant_tables(),
+        *constant_tables(),
     )
     vmem = pl.BlockSpec(memory_space=pltpu.VMEM)
     hbm = pl.BlockSpec(memory_space=pltpu.HBM)
@@ -439,17 +468,17 @@
         functools.partial(exchange, sectors, slabs, owned),
         out_shape=(
             pltpu.VMEM((tiles, 5, 64, 128), F32),
-            pltpu.VMEM((4, 80, slots), F32),
-            pltpu.VMEM((4, elems, slots), BF),
-            pltpu.VMEM((8, width), F32),
+            pltpu.VMEM((owned,), F32),
         ),
         in_specs=[hbm] * INPUTS,
-        out_specs=(vmem,) * 4,
+        out_specs=(vmem,) * 2,
         scratch_shapes=[pltpu.VMEM((tiles, 5, 64, 128), F32)]
         + [pltpu.VMEM(a.shape, a.dtype) for a in operands[1:]]
         + [
             pltpu.VMEM((960, elems), BF),
             pltpu.VMEM((6, 160, elems), BF),
+            pltpu.VMEM((4, elems, slots), BF),
+            pltpu.VMEM((4, 80, slots), F32),
             pltpu.VMEM((4, 80, slots), F32),
             pltpu.VMEM((320, 1024), BF),
             pltpu.VMEM((25, 6, 128), F32),
@@ -457,6 +486,7 @@
             pltpu.VMEM((2, 8, width), F32),
             pltpu.SemaphoreType.DMA((6,)),
             pltpu.SemaphoreType.DMA((6,)),
+            pltpu.SemaphoreType.REGULAR,
             pltpu.SemaphoreType.DMA((INPUTS,)),
             pltpu.SemaphoreType.DMA((5 * tiles,)),
         ],
@@ -470,11 +500,9 @@
             jax.ShapeDtypeStruct(adjoint.shape, F32),
             jax.ShapeDtypeStruct((owned,), F32),
         ),
-        in_specs=[vmem] * 4,
+        in_specs=[vmem] * 2,
         out_specs=(hbm, hbm),
         scratch_shapes=[
-            pltpu.VMEM((tiles, 5, 64, 128), F32),
-            pltpu.VMEM((owned,), F32),
             pltpu.SemaphoreType.DMA((tiles + 1,)),
         ],
         compiler_params=pltpu.CompilerParams(vmem_limit_bytes=40 * 1024 * 1024),

time: 14.7 us -> 12.6 us (0.86)
  the two profiles are of different devices: /device:TPU:0 before, /device:TPU:27 now
where the time goes in v3:
time: 12.6 us; the launch traced here: 12.4 us
  Pallas kernels  11.8 us (94%)
  between operations  0.64 us (5%)
    pallas_call x1, Pallas kernels, on_device(): pl.pallas_call(functools.partial(exchange, sectors, slabs, owned), out_sh...  10.6 us
    pallas_call x1, Pallas kernels, on_device(): pl.pallas_call(finish, out_shape=(jax.ShapeDtypeStruct(adjoint.shape, F32...  1.13 us

profile of v3, /device:TPU:27, one launch (start us, length us, event | category | flops | bytes accessed | tf_op | source)
XLA Modules:
  0.0 12.4 jit_solution(12992007223779971314)
XLA Ops:
  0.6 10.6 %shard_map.149 = (f32[8,5,64,128]{3,2,1,0:T(8,128)S(1)}, f32[128]{0:T(128)S(1)}) custom-call(f32[5,64,1024]{2,1,0:T(8,128)} %refs_0_.1, bf16[3,64,1024]{2,1,0:T(8,128)(2,1)} %refs_1_.1, f32[1,1024]{1,0:T(1,128)} %bitcast.10, f32[1,1024]{1,0:T(1,128)} %bitcast.11, f32[5,3,5]{2,1,0:T(4,128)} %bitcast.9, f32[5,6,5]{2,1,0:T(8,128)} %bitcast.7, ...), custom_call_target="tpu_custom_call" | custom-call | tf_op jit(solution)/shard_map/pallas_call | solution.py:467
  11.3 1.1 %shard_map.150 = (f32[5,64,1024]{2,1,0:T(8,128)}, f32[128]{0:T(128)}) custom-call(f32[8,5,64,128]{3,2,1,0:T(8,128)S(1)} %get-tuple-element.4.acc_ref, f32[128]{0:T(128)S(1)} %get-tuple-element.5.sums_ref), custom_call_target="tpu_custom_call" | custom-call | tf_op jit(solution)/shard_map/pallas_call | solution.py:497

commit v4 on v3

--- a/solution.py
+++ b/solution.py
@@ -171,11 +171,11 @@
         for h in (1, 2, 3, 0, 4)
         for t in range(tiles)
     }
-    for k in (1, 13, 2, 3, 11):
+    for k in (9, 6):
         loads[k].start()
     for key in fields:
         fields[key].start()
-    for k in (8, 9, 10, 6, 7, 12, 4, 5):
+    for k in (8, 10, 1, 13, 2, 3, 11, 7, 12, 4, 5):
         loads[k].start()
 
     sec = lax.axis_index("sector")
@@ -207,11 +207,103 @@
     def _():
         greet(dev_next)
 
+    def remote(src, dst, k, device):
+        return pltpu.make_async_remote_copy(
+            src_ref=src,
+            dst_ref=dst,
+            send_sem=send_sem.at[k],
+            recv_sem=recv_sem.at[k],
+            device_id=device,
+            device_id_type=MESH,
+        )
+
+    up_x = remote(send_ref.at[1], recv_ref.at[0], 0, dev_high)
+    down_x = remote(send_ref.at[0], recv_ref.at[1], 1, dev_low)
+    up_z = remote(send_ref.at[3], recv_ref.at[2], 2, dev_next)
+    down_z = remote(send_ref.at[2], recv_ref.at[3], 3, dev_prev)
+    up_b = remote(bsend_ref.at[2], brecv_ref.at[0], 4, dev_next)
+    down_b = remote(bsend_ref.at[0], brecv_ref.at[1], 5, dev_prev)
+
+    slot_ids = lax.broadcasted_iota(jnp.int32, (1, slots), 1)
+    rows_slots = lax.broadcasted_iota(jnp.int32, (elems, slots), 0).astype(jnp.int16)
+
+    def find_slots(i, ids):
+        ids = jnp.broadcast_to(ids, (elems, slots)).astype(jnp.int16)
+        oh_ref[i] = one_hot(rows_slots == ids)
+
+    def take_trace(t, face):
+        lanes = slice(128 * t, 128 * t + 128)
+        for c in range(5):
+            hi, lo = split2(face_rows(x_ref, t, c, face))
+            tr_ref[face, 16 * c : 16 * c + 16, lanes] = hi
+            tr_ref[face, 80 + 16 * c : 96 + 16 * c, lanes] = lo
+
+    def fill_send(i):
+        face = SIDES[i]
+        for t in range(tiles):
+            take_trace(t, face)
+        both = dot(tr_ref[face], oh_ref[i])
+        both = both[:80] + both[80:]
+        for n in range(0, slots, 128):
+            parts = [both[16 * h : 16 * h + 16, n : n + 128] for h in range(5)]
+            for c in range(5):
+                value = mixed(coef_ref, face + 1 - 2 * (face % 2), c, parts)
+                send_ref[i, 16 * c : 16 * c + 16, n : n + 128] = value
+
+    loads[9].wait()
+    for i in (2, 3):
+        find_slots(i, aslots_ref[i - 2 : i - 1, :])
+    loads[6].wait()
+    for c in range(5):
+        for h in range(5):
+            coef_ref[5 * c + h] = jnp.broadcast_to(0.1 * nbrmat_ref[c][:, h : h + 1], (6, 128))
+    for key in fields:
+        fields[key].wait()
+    fill_send(2)
+    fill_send(3)
+
+    @pl.when(has_low)
+    def _():
+        pl.semaphore_wait(barrier, 4)
+
+    @pl.when(jnp.logical_not(has_low))
+    def _():
+        pl.semaphore_wait(barrier, 3)
+        greet(dev_prev)
+
+    @pl.when(jnp.logical_not(has_high))
+    def _():
+        pl.semaphore_signal(far_sem, inc=1, device_id=dev_next, device_id_type=MESH)
+
+
+    @pl.when(has_high)
+    def _():
+        up_z.start()
+
+    @pl.when(has_low)
+    def _():
+        down_z.start()
+
+    @pl.when(jnp.logical_not(has_low))
+    def _():
+        recv_ref[2] = jnp.zeros((80, slots), F32)
+
+    @pl.when(jnp.logical_not(has_high))
+    def _():
+        recv_ref[3] = jnp.zeros((80, slots), F32)
+
+    loads[8].wait()
+    loads[10].wait()
+    for i in (0, 1):
+        live = slot_ids < live_ref[:, i : i + 1]
+        find_slots(i, jnp.where(live, sslots_ref[i : i + 1, :], -1))
+    fill_send(0)
+    fill_send(1)
+    up_x.start()
+    down_x.start()
+
     for k in (1, 13, 2, 3, 11):
         loads[k].wait()
-    for h in (1, 2, 3):
-        for t in range(tiles):
-            fields[t, h].wait()
     parts = []
     for t in range(tiles):
         lanes = slice(128 * t, 128 * t + 128)
@@ -238,95 +330,11 @@
         sums = dot_nt(stack, one_hot(rows_blk == ids))
         total = jnp.sum(sums, axis=0, keepdims=True)
         bsend_ref[j] = jnp.broadcast_to(total, (8, width))
-    def remote(src, dst, k, device):
-        return pltpu.make_async_remote_copy(
-            src_ref=src,
-            dst_ref=dst,
-            send_sem=send_sem.at[k],
-            recv_sem=recv_sem.at[k],
-            device_id=device,
-            device_id_type=MESH,
-        )
-
-    up_x = remote(send_ref.at[1], recv_ref.at[0], 0, dev_high)
-    down_x = remote(send_ref.at[0], recv_ref.at[1], 1, dev_low)
-    up_z = remote(send_ref.at[3], recv_ref.at[2], 2, dev_next)
-    down_z = remote(send_ref.at[2], recv_ref.at[3], 3, dev_prev)
-    up_b = remote(bsend_ref.at[2], brecv_ref.at[0], 4, dev_next)
-    down_b = remote(bsend_ref.at[0], brecv_ref.at[1], 5, dev_prev)
+    up_b.start()
 
     @pl.when(has_low)
     def _():
-        pl.semaphore_wait(barrier, 4)
         down_b.start()
-
-    @pl.when(jnp.logical_not(has_low))
-    def _():
-        pl.semaphore_wait(barrier, 3)
-        greet(dev_prev)
-
-    @pl.when(jnp.logical_not(has_high))
-    def _():
-        pl.semaphore_signal(far_sem, inc=1, device_id=dev_next, device_id_type=MESH)
-
-    up_b.start()
-    for k in (8, 9, 10, 6):
-        loads[k].wait()
-    slot_ids = lax.broadcasted_iota(jnp.int32, (1, slots), 1)
-    rows_slots = lax.broadcasted_iota(jnp.int32, (elems, slots), 0).astype(jnp.int16)
-    for i in range(4):
-        row = i % 2
-        ids = (sslots_ref if i < 2 else aslots_ref)[row : row + 1, :]
-        if i < 2:
-            ids = jnp.where(slot_ids < live_ref[:, row : row + 1], ids, -1)
-        ids = jnp.broadcast_to(ids, (elems, slots)).astype(jnp.int16)
-        oh_ref[i] = one_hot(rows_slots == ids)
-
-    for c in range(5):
-        for h in range(5):
-            coef_ref[5 * c + h] = jnp.broadcast_to(0.1 * nbrmat_ref[c][:, h : h + 1], (6, 128))
-
-    def take_trace(t, face):
-        lanes = slice(128 * t, 128 * t + 128)
-        for c in range(5):
-            hi, lo = split2(face_rows(x_ref, t, c, face))
-            tr_ref[face, 16 * c : 16 * c + 16, lanes] = hi
-            tr_ref[face, 80 + 16 * c : 96 + 16 * c, lanes] = lo
-
-    for h in (0, 4):
-        for t in range(tiles):
-            fields[t, h].wait()
-    for t in range(tiles):
-        for face in SIDES:
-            take_trace(t, face)
-
-    for i, face in enumerate(SIDES):
-        both = dot(tr_ref[face], oh_ref[i])
-        both = both[:80] + both[80:]
-        for n in range(0, slots, 128):
-            parts = [both[16 * h : 16 * h + 16, n : n + 128] for h in range(5)]
-            for c in range(5):
-                value = mixed(coef_ref, face + 1 - 2 * (face % 2), c, parts)
-                send_ref[i, 16 * c : 16 * c + 16, n : n + 128] = value
-
-    up_x.start()
-    down_x.start()
-
-    @pl.when(has_high)
-    def _():
-        up_z.start()
-
-    @pl.when(has_low)
-    def _():
-        down_z.start()
-
-    @pl.when(jnp.logical_not(has_low))
-    def _():
-        recv_ref[2] = jnp.zeros((80, slots), F32)
-
-    @pl.when(jnp.logical_not(has_high))
-    def _():
-        recv_ref[3] = jnp.zeros((80, slots), F32)
 
     for k in (7, 12, 4, 5):
         loads[k].wait()
@@ -374,7 +382,7 @@
             acc_ref[t, c] = scaled + own[64 * c : 64 * c + 64, lanes]
 
     rows_src = lax.broadcasted_iota(jnp.int32, (elems, elems), 0).astype(jnp.int16)
-    for f in range(6):
+    def gather(f):
         g = f + 1 - 2 * (f % 2)
         ids = jnp.broadcast_to(nbr_ref[f : f + 1, :], (elems, elems)).astype(jnp.int16)
         both = dot(tr_ref[g], one_hot(rows_src == ids))
@@ -383,10 +391,16 @@
             parts = [both[16 * h : 16 * h + 16, 128 * t : 128 * t + 128] for h in range(5)]
             add_face(acc_ref, t, f, [mixed(coef_ref, f, c, parts) for c in range(5)])
 
+    for f in (0, 1, 2):
+        gather(f)
+
     @pl.when(jnp.logical_not(has_low))
     def _():
         pl.semaphore_wait(far_sem, 1)
         down_b.start()
+
+    for f in (3, 4, 5):
+        gather(f)
 
     up_x.wait()
     down_x.wait()

time: 12.6 us -> 13.5 us (1.071)
  the two profiles are of different devices: /device:TPU:27 before, /device:TPU:0 now
where the time goes in v4:
time: 13.5 us; the launch traced here: 13.3 us
  Pallas kernels  12.7 us (94%)
  between operations  0.64 us (5%)
    pallas_call x1, Pallas kernels, on_device(): pl.pallas_call(functools.partial(exchange, sectors, slabs, owned), out_sh...  11.5 us
    pallas_call x1, Pallas kernels, on_device(): pl.pallas_call(finish, out_shape=(jax.ShapeDtypeStruct(adjoint.shape, F32...  1.13 us

profile of v4, /device:TPU:0, one launch (start us, length us, event | category | flops | bytes accessed | tf_op | source)
XLA Modules:
  0.0 13.3 jit_solution(15757772568518083665)
XLA Ops:
  0.6 11.5 %shard_map.149 = (f32[8,5,64,128]{3,2,1,0:T(8,128)S(1)}, f32[128]{0:T(128)S(1)}) custom-call(f32[5,64,1024]{2,1,0:T(8,128)} %refs_0_.1, bf16[3,64,1024]{2,1,0:T(8,128)(2,1)} %refs_1_.1, f32[1,1024]{1,0:T(1,128)} %bitcast.10, f32[1,1024]{1,0:T(1,128)} %bitcast.11, f32[5,3,5]{2,1,0:T(4,128)} %bitcast.9, f32[5,6,5]{2,1,0:T(8,128)} %bitcast.7, ...), custom_call_target="tpu_custom_call" | custom-call | tf_op jit(solution)/shard_map/pallas_call | solution.py:481
  12.2 1.1 %shard_map.150 = (f32[5,64,1024]{2,1,0:T(8,128)}, f32[128]{0:T(128)}) custom-call(f32[8,5,64,128]{3,2,1,0:T(8,128)S(1)} %get-tuple-element.4.acc_ref, f32[128]{0:T(128)S(1)} %get-tuple-element.5.sums_ref), custom_call_target="tpu_custom_call" | custom-call | tf_op jit(solution)/shard_map/pallas_call | solution.py:511

commit v5 on v4

--- a/solution.py
+++ b/solution.py
@@ -198,10 +198,7 @@
 
     greet(dev_low)
     greet(dev_high)
-
-    @pl.when(has_low)
-    def _():
-        greet(dev_prev)
+    greet(dev_prev)
 
     @pl.when(has_high)
     def _():
@@ -269,12 +266,10 @@
     @pl.when(jnp.logical_not(has_low))
     def _():
         pl.semaphore_wait(barrier, 3)
-        greet(dev_prev)
 
     @pl.when(jnp.logical_not(has_high))
     def _():
         pl.semaphore_signal(far_sem, inc=1, device_id=dev_next, device_id_type=MESH)
-
 
     @pl.when(has_high)
     def _():

time: 13.5 us -> 13.4 us (level)
  no operation moved by 1% of the time
where the time goes in v5:
time: 13.4 us; the launch traced here: 13.2 us
  Pallas kernels  12.6 us (94%)
  between operations  0.64 us (5%)
    pallas_call x1, Pallas kernels, on_device(): pl.pallas_call(functools.partial(exchange, sectors, slabs, owned), out_sh...  11.5 us
    pallas_call x1, Pallas kernels, on_device(): pl.pallas_call(finish, out_shape=(jax.ShapeDtypeStruct(adjoint.shape, F32...  1.13 us

profile of v5, /device:TPU:0, one launch (start us, length us, event | category | flops | bytes accessed | tf_op | source)
XLA Modules:
  0.0 13.2 jit_solution(8105269883902653352)
XLA Ops:
  0.6 11.5 %shard_map.149 = (f32[8,5,64,128]{3,2,1,0:T(8,128)S(1)}, f32[128]{0:T(128)S(1)}) custom-call(f32[5,64,1024]{2,1,0:T(8,128)} %refs_0_.1, bf16[3,64,1024]{2,1,0:T(8,128)(2,1)} %refs_1_.1, f32[1,1024]{1,0:T(1,128)} %bitcast.10, f32[1,1024]{1,0:T(1,128)} %bitcast.11, f32[5,3,5]{2,1,0:T(4,128)} %bitcast.9, f32[5,6,5]{2,1,0:T(8,128)} %bitcast.7, ...), custom_call_target="tpu_custom_call" | custom-call | tf_op jit(solution)/shard_map/pallas_call | solution.py:476
  12.1 1.1 %shard_map.150 = (f32[5,64,1024]{2,1,0:T(8,128)}, f32[128]{0:T(128)}) custom-call(f32[8,5,64,128]{3,2,1,0:T(8,128)S(1)} %get-tuple-element.4.acc_ref, f32[128]{0:T(128)S(1)} %get-tuple-element.5.sums_ref), custom_call_target="tpu_custom_call" | custom-call | tf_op jit(solution)/shard_map/pallas_call | solution.py:506

commit v6 on v5

--- a/solution.py
+++ b/solution.py
@@ -256,20 +256,54 @@
             coef_ref[5 * c + h] = jnp.broadcast_to(0.1 * nbrmat_ref[c][:, h : h + 1], (6, 128))
     for key in fields:
         fields[key].wait()
+    def sum_blocks():
+        for k in (1, 13, 2, 3, 11):
+            loads[k].wait()
+        parts = []
+        for t in range(tiles):
+            lanes = slice(128 * t, 128 * t + 128)
+            total = x_ref[t, 1] * vel_ref[0, :, lanes].astype(F32)
+            total += x_ref[t, 2] * vel_ref[1, :, lanes].astype(F32)
+            total += x_ref[t, 3] * vel_ref[2, :, lanes].astype(F32)
+            parts.append(jnp.sum(total * weight_ref[...], axis=0, keepdims=True))
+        elem_grad = drag_ref[...] * jnp.concatenate(parts, axis=1)
+        weighted = bw_ref[...] * elem_grad
+        w1 = weighted.astype(BF)
+        rest = weighted - w1.astype(F32)
+        w2 = rest.astype(BF)
+        w3 = (rest - w2.astype(F32)).astype(BF).astype(F32)
+        row16 = lax.broadcasted_iota(jnp.int32, (16, elems), 0)
+        stack = jnp.where(row16 == 0, w1.astype(F32), 0.0)
+        stack = jnp.where(row16 == 1, w2.astype(F32), stack)
+        stack = jnp.where(row16 == 2, w3, stack).astype(BF)
+        rel = eb_ref[...] - (joint - 1) * owned
+        rel = jnp.where(rel < 0, rel + BLOCKS, rel)
+        rel = jnp.where(rel >= BLOCKS, rel - BLOCKS, rel)
+        rows_blk = lax.broadcasted_iota(jnp.int32, (width, elems), 0).astype(jnp.int16)
+        for j in range(3):
+            ids = jnp.broadcast_to(rel - j * owned, (width, elems)).astype(jnp.int16)
+            sums = dot_nt(stack, one_hot(rows_blk == ids))
+            total = jnp.sum(sums, axis=0, keepdims=True)
+            bsend_ref[j] = jnp.broadcast_to(total, (8, width))
+
+    @pl.when(jnp.logical_not(has_high))
+    def _():
+        sum_blocks()
+        pl.semaphore_wait(barrier, 4)
+        pl.semaphore_signal(far_sem, inc=1, device_id=dev_next, device_id_type=MESH)
+        up_b.start()
+        down_b.start()
+
     fill_send(2)
     fill_send(3)
 
-    @pl.when(has_low)
+    @pl.when(jnp.logical_and(has_low, has_high))
     def _():
         pl.semaphore_wait(barrier, 4)
 
     @pl.when(jnp.logical_not(has_low))
     def _():
         pl.semaphore_wait(barrier, 3)
-
-    @pl.when(jnp.logical_not(has_high))
-    def _():
-        pl.semaphore_signal(far_sem, inc=1, device_id=dev_next, device_id_type=MESH)
 
     @pl.when(has_high)
     def _():
@@ -297,37 +331,12 @@
     up_x.start()
     down_x.start()
 
-    for k in (1, 13, 2, 3, 11):
-        loads[k].wait()
-    parts = []
-    for t in range(tiles):
-        lanes = slice(128 * t, 128 * t + 128)
-        total = x_ref[t, 1] * vel_ref[0, :, lanes].astype(F32)
-        total += x_ref[t, 2] * vel_ref[1, :, lanes].astype(F32)
-        total += x_ref[t, 3] * vel_ref[2, :, lanes].astype(F32)
-        parts.append(jnp.sum(total * weight_ref[...], axis=0, keepdims=True))
-    elem_grad = drag_ref[...] * jnp.concatenate(parts, axis=1)
-    weighted = bw_ref[...] * elem_grad
-    w1 = weighted.astype(BF)
-    rest = weighted - w1.astype(F32)
-    w2 = rest.astype(BF)
-    w3 = (rest - w2.astype(F32)).astype(BF).astype(F32)
-    row16 = lax.broadcasted_iota(jnp.int32, (16, elems), 0)
-    stack = jnp.where(row16 == 0, w1.astype(F32), 0.0)
-    stack = jnp.where(row16 == 1, w2.astype(F32), stack)
-    stack = jnp.where(row16 == 2, w3, stack).astype(BF)
-    rel = eb_ref[...] - (joint - 1) * owned
-    rel = jnp.where(rel < 0, rel + BLOCKS, rel)
-    rel = jnp.where(rel >= BLOCKS, rel - BLOCKS, rel)
-    rows_blk = lax.broadcasted_iota(jnp.int32, (width, elems), 0).astype(jnp.int16)
-    for j in range(3):
-        ids = jnp.broadcast_to(rel - j * owned, (width, elems)).astype(jnp.int16)
-        sums = dot_nt(stack, one_hot(rows_blk == ids))
-        total = jnp.sum(sums, axis=0, keepdims=True)
-        bsend_ref[j] = jnp.broadcast_to(total, (8, width))
-    up_b.start()
-
-    @pl.when(has_low)
+    @pl.when(has_high)
+    def _():
+        sum_blocks()
+        up_b.start()
+
+    @pl.when(jnp.logical_and(has_low, has_high))
     def _():
         down_b.start()
 

time: 13.4 us -> 13.4 us (level)
  no operation moved by 1% of the time
where the time goes in v6:
time: 13.4 us; the launch traced here: 13.2 us
  Pallas kernels  12.6 us (94%)
  between operations  0.64 us (5%)
    pallas_call x1, Pallas kernels, on_device(): pl.pallas_call(functools.partial(exchange, sectors, slabs, owned), out_sh...  11.4 us
    pallas_call x1, Pallas kernels, on_device(): pl.pallas_call(finish, out_shape=(jax.ShapeDtypeStruct(adjoint.shape, F32...  1.13 us

profile of v6, /device:TPU:0, one launch (start us, length us, event | category | flops | bytes accessed | tf_op | source)
XLA Modules:
  0.0 13.2 jit_solution(14408636954800835966)
XLA Ops:
  0.6 11.4 %shard_map.149 = (f32[8,5,64,128]{3,2,1,0:T(8,128)S(1)}, f32[128]{0:T(128)S(1)}) custom-call(f32[5,64,1024]{2,1,0:T(8,128)} %refs_0_.1, bf16[3,64,1024]{2,1,0:T(8,128)(2,1)} %refs_1_.1, f32[1,1024]{1,0:T(1,128)} %bitcast.10, f32[1,1024]{1,0:T(1,128)} %bitcast.11, f32[5,3,5]{2,1,0:T(4,128)} %bitcast.9, f32[5,6,5]{2,1,0:T(8,128)} %bitcast.7, ...), custom_call_target="tpu_custom_call" | custom-call | tf_op jit(solution)/shard_map/pallas_call | solution.py:485
  12.1 1.1 %shard_map.150 = (f32[5,64,1024]{2,1,0:T(8,128)}, f32[128]{0:T(128)}) custom-call(f32[8,5,64,128]{3,2,1,0:T(8,128)S(1)} %get-tuple-element.4.acc_ref, f32[128]{0:T(128)S(1)} %get-tuple-element.5.sums_ref), custom_call_target="tpu_custom_call" | custom-call | tf_op jit(solution)/shard_map/pallas_call | solution.py:515

commit v7 on v6

--- a/solution.py
+++ b/solution.py
@@ -142,6 +142,7 @@
         xs_ref,
         tr_ref,
         oh_ref,
+        place_ref,
         send_ref,
         recv_ref,
         a_ref,
@@ -171,11 +172,11 @@
         for h in (1, 2, 3, 0, 4)
         for t in range(tiles)
     }
-    for k in (9, 6):
+    for k in (9, 8, 10):
         loads[k].start()
     for key in fields:
         fields[key].start()
-    for k in (8, 10, 1, 13, 2, 3, 11, 7, 12, 4, 5):
+    for k in (6, 1, 13, 2, 3, 11, 7, 12, 4, 5):
         loads[k].start()
 
     sec = lax.axis_index("sector")
@@ -224,9 +225,21 @@
     slot_ids = lax.broadcasted_iota(jnp.int32, (1, slots), 1)
     rows_slots = lax.broadcasted_iota(jnp.int32, (elems, slots), 0).astype(jnp.int16)
 
-    def find_slots(i, ids):
-        ids = jnp.broadcast_to(ids, (elems, slots)).astype(jnp.int16)
+    columns = lax.broadcasted_iota(jnp.int32, (slots, elems), 1).astype(jnp.int16)
+
+    def slot_row(i):
+        if i >= 2:
+            return aslots_ref[i - 2 : i - 1, :]
+        return jnp.where(slot_ids < live_ref[:, i : i + 1], sslots_ref[i : i + 1, :], -1)
+
+    def find_slots(i):
+        ids = jnp.broadcast_to(slot_row(i), (elems, slots)).astype(jnp.int16)
         oh_ref[i] = one_hot(rows_slots == ids)
+
+    def find_places(i):
+        ids = jnp.broadcast_to(slot_row(i), (128, slots)).T
+        ids = jnp.concatenate([ids] * tiles, axis=1).astype(jnp.int16)
+        place_ref[i] = one_hot(columns == ids)
 
     def take_trace(t, face):
         lanes = slice(128 * t, 128 * t + 128)
@@ -240,20 +253,12 @@
         for t in range(tiles):
             take_trace(t, face)
         both = dot(tr_ref[face], oh_ref[i])
-        both = both[:80] + both[80:]
-        for n in range(0, slots, 128):
-            parts = [both[16 * h : 16 * h + 16, n : n + 128] for h in range(5)]
-            for c in range(5):
-                value = mixed(coef_ref, face + 1 - 2 * (face % 2), c, parts)
-                send_ref[i, 16 * c : 16 * c + 16, n : n + 128] = value
-
-    loads[9].wait()
-    for i in (2, 3):
-        find_slots(i, aslots_ref[i - 2 : i - 1, :])
-    loads[6].wait()
-    for c in range(5):
-        for h in range(5):
-            coef_ref[5 * c + h] = jnp.broadcast_to(0.1 * nbrmat_ref[c][:, h : h + 1], (6, 128))
+        send_ref[i] = both[:80] + both[80:]
+
+    for k in (9, 8, 10):
+        loads[k].wait()
+    for i in range(4):
+        find_slots(i)
     for key in fields:
         fields[key].wait()
     def sum_blocks():
@@ -305,11 +310,13 @@
     def _():
         pl.semaphore_wait(barrier, 3)
 
-    @pl.when(has_high)
+    even = axi % 2 == 0
+
+    @pl.when(jnp.logical_and(has_high, even))
     def _():
         up_z.start()
 
-    @pl.when(has_low)
+    @pl.when(jnp.logical_and(has_low, jnp.logical_not(even)))
     def _():
         down_z.start()
 
@@ -321,16 +328,19 @@
     def _():
         recv_ref[3] = jnp.zeros((80, slots), F32)
 
-    loads[8].wait()
-    loads[10].wait()
-    for i in (0, 1):
-        live = slot_ids < live_ref[:, i : i + 1]
-        find_slots(i, jnp.where(live, sslots_ref[i : i + 1, :], -1))
     fill_send(0)
     fill_send(1)
     up_x.start()
     down_x.start()
 
+    @pl.when(jnp.logical_and(has_high, jnp.logical_not(even)))
+    def _():
+        up_z.start()
+
+    @pl.when(jnp.logical_and(has_low, even))
+    def _():
+        down_z.start()
+
     @pl.when(has_high)
     def _():
         sum_blocks()
@@ -340,8 +350,13 @@
     def _():
         down_b.start()
 
-    for k in (7, 12, 4, 5):
+    for k in (7, 12, 4, 5, 6):
         loads[k].wait()
+    for c in range(5):
+        for h in range(5):
+            coef_ref[5 * c + h] = jnp.broadcast_to(0.1 * nbrmat_ref[c][:, h : h + 1], (6, 128))
+    for i in range(4):
+        find_places(i)
 
     spread = jnp.minimum(lax.broadcasted_iota(jnp.int32, (5, 384), 1) // 64, 4)
     spread = jnp.where(spread == lax.broadcasted_iota(jnp.int32, (5, 384), 0), 1.0, 0.0)
@@ -368,15 +383,13 @@
         lanes = slice(128 * t, 128 * t + 128)
         for h in range(5):
             hi, lo = split2(x_ref[t, h])
-            places = ((768, hi), (832, lo), (896, hi))
-            if h < 4:
-                places = ((64 * h, hi), (256 + 64 * h, lo), (512 + 64 * h, hi))
-            for base, part in places:
-                xs_ref[base : base + 64, lanes] = part
+            for base, part in ((0, hi), (256, lo)) if h < 4 else ((256, hi), (320, lo)):
+                xs_ref[64 * h + base : 64 * h + base + 64, lanes] = part
         for face in (2, 3):
             take_trace(t, face)
 
-    own = dot(a_ref[:, 0:960], xs_ref[...])
+    xs = [xs_ref[rows, :] for rows in (slice(0, 512), slice(0, 256), slice(512, 640), slice(512, 576))]
+    own = dot(a_ref[:, 0:960], jnp.concatenate(xs, axis=0))
     keep = 1.0 - 0.1 * drag_ref[...]
     for t in range(tiles):
         lanes = slice(128 * t, 128 * t + 128)
@@ -386,28 +399,32 @@
             acc_ref[t, c] = scaled + own[64 * c : 64 * c + 64, lanes]
 
     rows_src = lax.broadcasted_iota(jnp.int32, (elems, elems), 0).astype(jnp.int16)
-    def gather(f):
+    def gather(f, i=None):
         g = f + 1 - 2 * (f % 2)
         ids = jnp.broadcast_to(nbr_ref[f : f + 1, :], (elems, elems)).astype(jnp.int16)
-        both = dot(tr_ref[g], one_hot(rows_src == ids))
+        sources, places = tr_ref[g], one_hot(rows_src == ids)
+        if i is not None:
+            got = jnp.concatenate(split2(recv_ref[i]), axis=0)
+            sources = jnp.concatenate([sources, got], axis=1)
+            places = jnp.concatenate([places, place_ref[i]], axis=0)
+        both = dot(sources, places)
         both = both[:80] + both[80:]
         for t in range(tiles):
             parts = [both[16 * h : 16 * h + 16, 128 * t : 128 * t + 128] for h in range(5)]
             add_face(acc_ref, t, f, [mixed(coef_ref, f, c, parts) for c in range(5)])
 
-    for f in (0, 1, 2):
-        gather(f)
+    gather(2)
+    gather(3)
 
     @pl.when(jnp.logical_not(has_low))
     def _():
         pl.semaphore_wait(far_sem, 1)
         down_b.start()
 
-    for f in (3, 4, 5):
-        gather(f)
-
     up_x.wait()
     down_x.wait()
+    gather(0, 0)
+    gather(1, 1)
 
     @pl.when(has_high)
     def _():
@@ -419,12 +436,8 @@
         down_z.wait_send()
         up_z.wait_recv()
 
-    for i, face in enumerate(SIDES):
-        both = dot_nt(jnp.concatenate(split2(recv_ref[i]), axis=0), oh_ref[i])
-        both = both[:80] + both[80:]
-        for t in range(tiles):
-            lanes = slice(128 * t, 128 * t + 128)
-            add_face(acc_ref, t, face, [both[16 * c : 16 * c + 16, lanes] for c in range(5)])
+    gather(4, 2)
+    gather(5, 3)
 
     up_b.wait()
     down_b.wait()
@@ -493,9 +506,10 @@
         scratch_shapes=[pltpu.VMEM((tiles, 5, 64, 128), F32)]
         + [pltpu.VMEM(a.shape, a.dtype) for a in operands[1:]]
         + [
-            pltpu.VMEM((960, elems), BF),
+            pltpu.VMEM((640, elems), BF),
             pltpu.VMEM((6, 160, elems), BF),
             pltpu.VMEM((4, elems, slots), BF),
+            pltpu.VMEM((4, slots, elems), BF),
             pltpu.VMEM((4, 80, slots), F32),
             pltpu.VMEM((4, 80, slots), F32),
             pltpu.VMEM((320, 1024), BF),

time: 13.4 us -> 13.4 us (level)
  no operation moved by 1% of the time
where the time goes in v7:
time: 13.4 us; the launch traced here: 13.2 us
  Pallas kernels  12.6 us (94%)
  between operations  0.64 us (5%)
    pallas_call x1, Pallas kernels, on_device(): pl.pallas_call(functools.partial(exchange, sectors, slabs, owned), out_sh...  11.5 us
    pallas_call x1, Pallas kernels, on_device(): pl.pallas_call(finish, out_shape=(jax.ShapeDtypeStruct(adjoint.shape, F32...  1.13 us

profile of v7, /device:TPU:0, one launch (start us, length us, event | category | flops | bytes accessed | tf_op | source)
XLA Modules:
  0.0 13.2 jit_solution(12317486125323822241)
XLA Ops:
  0.6 11.5 %shard_map.149 = (f32[8,5,64,128]{3,2,1,0:T(8,128)S(1)}, f32[128]{0:T(128)S(1)}) custom-call(f32[5,64,1024]{2,1,0:T(8,128)} %refs_0_.1, bf16[3,64,1024]{2,1,0:T(8,128)(2,1)} %refs_1_.1, f32[1,1024]{1,0:T(1,128)} %bitcast.10, f32[1,1024]{1,0:T(1,128)} %bitcast.11, f32[5,3,5]{2,1,0:T(4,128)} %bitcast.9, f32[5,6,5]{2,1,0:T(8,128)} %bitcast.7, ...), custom_call_target="tpu_custom_call" | custom-call | tf_op jit(solution)/shard_map/pallas_call | solution.py:498
  12.1 1.1 %shard_map.150 = (f32[5,64,1024]{2,1,0:T(8,128)}, f32[128]{0:T(128)}) custom-call(f32[8,5,64,128]{3,2,1,0:T(8,128)S(1)} %get-tuple-element.4.acc_ref, f32[128]{0:T(128)S(1)} %get-tuple-element.5.sums_ref), custom_call_target="tpu_custom_call" | custom-call | tf_op jit(solution)/shard_map/pallas_call | solution.py:529

commit v8 on v7

--- a/solution.py
+++ b/solution.py
@@ -72,15 +72,15 @@
     return jnp.where(mask, jnp.ones((), BF), jnp.zeros((), BF))
 
 
-def add_face(ref, tile, face, part):
+def add_face(ref, tile, face, part, axial):
     low = lax.broadcasted_iota(jnp.int32, (8, 128), 0) < 4
     for c in range(5):
         rows = part[c]
-        if face < 2:
+        if axial:
+            ids = pl.ds(3 * (face - 4), 16, stride=4)
+            ref[tile, c, ids, :] = ref[tile, c, ids, :] + rows
+        elif face < 2:
             ids = pl.ds(48 * face, 16)
-            ref[tile, c, ids, :] = ref[tile, c, ids, :] + rows
-        elif face >= 4:
-            ids = pl.ds(3 * (face - 4), 16, stride=4)
             ref[tile, c, ids, :] = ref[tile, c, ids, :] + rows
         else:
             for v in range(2):
@@ -94,16 +94,16 @@
 
 
 def mixed(coef_ref, face, c, parts):
-    total = coef_ref[5 * c, face : face + 1, :] * parts[0]
+    total = coef_ref[5 * c, pl.ds(face, 1), :] * parts[0]
     for h in range(1, 5):
-        total += coef_ref[5 * c + h, face : face + 1, :] * parts[h]
+        total += coef_ref[5 * c + h, pl.ds(face, 1), :] * parts[h]
     return total
 
 
-def face_rows(ref, tile, c, face):
-    if face < 2:
+def face_rows(ref, tile, c, face, axial):
+    if not axial and face < 2:
         return ref[tile, c, 48 * face : 48 * face + 16, :]
-    if face >= 4:
+    if axial:
         return ref[tile, c, pl.ds(3 * (face - 4), 16, stride=4), :]
     low = lax.broadcasted_iota(jnp.int32, (8, 128), 0) < 4
     out = []
@@ -222,6 +222,14 @@
     up_b = remote(bsend_ref.at[2], brecv_ref.at[0], 4, dev_next)
     down_b = remote(bsend_ref.at[0], brecv_ref.at[1], 5, dev_prev)
 
+    @pl.when(jnp.logical_not(has_high))
+    def _():
+        pl.semaphore_wait(barrier, 4)
+        pl.semaphore_signal(far_sem, inc=1, device_id=dev_next, device_id_type=MESH)
+
+    even = axi % 2 == 0
+    first_face = 5 - axi % 2
+    second_face = 4 + axi % 2
     slot_ids = lax.broadcasted_iota(jnp.int32, (1, slots), 1)
     rows_slots = lax.broadcasted_iota(jnp.int32, (elems, slots), 0).astype(jnp.int16)
 
@@ -241,17 +249,17 @@
         ids = jnp.concatenate([ids] * tiles, axis=1).astype(jnp.int16)
         place_ref[i] = one_hot(columns == ids)
 
-    def take_trace(t, face):
+    def take_trace(t, face, axial=False):
         lanes = slice(128 * t, 128 * t + 128)
         for c in range(5):
-            hi, lo = split2(face_rows(x_ref, t, c, face))
+            hi, lo = split2(face_rows(x_ref, t, c, face, axial))
             tr_ref[face, 16 * c : 16 * c + 16, lanes] = hi
             tr_ref[face, 80 + 16 * c : 96 + 16 * c, lanes] = lo
 
-    def fill_send(i):
-        face = SIDES[i]
+    def fill_send(face, axial=False):
+        i = face - 2 if axial else face
         for t in range(tiles):
-            take_trace(t, face)
+            take_trace(t, face, axial)
         both = dot(tr_ref[face], oh_ref[i])
         send_ref[i] = both[:80] + both[80:]
 
@@ -294,13 +302,10 @@
     @pl.when(jnp.logical_not(has_high))
     def _():
         sum_blocks()
-        pl.semaphore_wait(barrier, 4)
-        pl.semaphore_signal(far_sem, inc=1, device_id=dev_next, device_id_type=MESH)
         up_b.start()
         down_b.start()
 
-    fill_send(2)
-    fill_send(3)
+    fill_send(first_face, True)
 
     @pl.when(jnp.logical_and(has_low, has_high))
     def _():
@@ -310,13 +315,21 @@
     def _():
         pl.semaphore_wait(barrier, 3)
 
-    even = axi % 2 == 0
-
     @pl.when(jnp.logical_and(has_high, even))
     def _():
         up_z.start()
 
     @pl.when(jnp.logical_and(has_low, jnp.logical_not(even)))
+    def _():
+        down_z.start()
+
+    fill_send(second_face, True)
+
+    @pl.when(jnp.logical_and(has_high, jnp.logical_not(even)))
+    def _():
+        up_z.start()
+
+    @pl.when(jnp.logical_and(has_low, even))
     def _():
         down_z.start()
 
@@ -332,14 +345,6 @@
     fill_send(1)
     up_x.start()
     down_x.start()
-
-    @pl.when(jnp.logical_and(has_high, jnp.logical_not(even)))
-    def _():
-        up_z.start()
-
-    @pl.when(jnp.logical_and(has_low, even))
-    def _():
-        down_z.start()
 
     @pl.when(has_high)
     def _():
@@ -399,9 +404,9 @@
             acc_ref[t, c] = scaled + own[64 * c : 64 * c + 64, lanes]
 
     rows_src = lax.broadcasted_iota(jnp.int32, (elems, elems), 0).astype(jnp.int16)
-    def gather(f, i=None):
-        g = f + 1 - 2 * (f % 2)
-        ids = jnp.broadcast_to(nbr_ref[f : f + 1, :], (elems, elems)).astype(jnp.int16)
+    def gather(f, i=None, axial=False):
+        g = 9 - f if axial else f + 1 - 2 * (f % 2)
+        ids = jnp.broadcast_to(nbr_ref[pl.ds(f, 1), :], (elems, elems)).astype(jnp.int16)
         sources, places = tr_ref[g], one_hot(rows_src == ids)
         if i is not None:
             got = jnp.concatenate(split2(recv_ref[i]), axis=0)
@@ -411,33 +416,47 @@
         both = both[:80] + both[80:]
         for t in range(tiles):
             parts = [both[16 * h : 16 * h + 16, 128 * t : 128 * t + 128] for h in range(5)]
-            add_face(acc_ref, t, f, [mixed(coef_ref, f, c, parts) for c in range(5)])
+            add_face(acc_ref, t, f, [mixed(coef_ref, f, c, parts) for c in range(5)], axial)
+
+    @pl.when(jnp.logical_not(has_low))
+    def _():
+        pl.semaphore_wait(far_sem, 1)
+        down_b.start()
 
     gather(2)
     gather(3)
-
-    @pl.when(jnp.logical_not(has_low))
-    def _():
-        pl.semaphore_wait(far_sem, 1)
-        down_b.start()
-
     up_x.wait()
     down_x.wait()
     gather(0, 0)
     gather(1, 1)
 
+    @pl.when(jnp.logical_and(has_high, even))
+    def _():
+        down_z.wait_recv()
+
+    @pl.when(jnp.logical_not(even))
+    def _():
+        up_z.wait_recv()
+
+    gather(first_face, first_face - 2, True)
+
+    @pl.when(jnp.logical_and(has_low, even))
+    def _():
+        up_z.wait_recv()
+
+    @pl.when(jnp.logical_and(has_high, jnp.logical_not(even)))
+    def _():
+        down_z.wait_recv()
+
+    gather(second_face, second_face - 2, True)
+
     @pl.when(has_high)
     def _():
         up_z.wait_send()
-        down_z.wait_recv()
 
     @pl.when(has_low)
     def _():
         down_z.wait_send()
-        up_z.wait_recv()
-
-    gather(4, 2)
-    gather(5, 3)
 
     up_b.wait()
     down_b.wait()

time: 13.4 us -> 13.6 us (1.015)
  Pallas kernels: 12.6 us -> 12.8 us
    pallas_call x1, Pallas kernels: 11.5 us -> 11.6 us  [on_device(): pl.pallas_call(functools.partial(exchange, sectors, slabs, owned), out_sh...]
where the time goes in v8:
time: 13.6 us; the launch traced here: 13.4 us
  Pallas kernels  12.8 us (94%)
  between operations  0.64 us (5%)
    pallas_call x1, Pallas kernels, on_device(): pl.pallas_call(functools.partial(exchange, sectors, slabs, owned), out_sh...  11.6 us
    pallas_call x1, Pallas kernels, on_device(): pl.pallas_call(finish, out_shape=(jax.ShapeDtypeStruct(adjoint.shape, F32...  1.13 us

profile of v8, /device:TPU:0, one launch (start us, length us, event | category | flops | bytes accessed | tf_op | source)
XLA Modules:
  0.0 13.4 jit_solution(1482097936987586337)
XLA Ops:
  0.6 11.6 %shard_map.149 = (f32[8,5,64,128]{3,2,1,0:T(8,128)S(1)}, f32[128]{0:T(128)S(1)}) custom-call(f32[5,64,1024]{2,1,0:T(8,128)} %refs_0_.1, bf16[3,64,1024]{2,1,0:T(8,128)(2,1)} %refs_1_.1, f32[1,1024]{1,0:T(1,128)} %bitcast.10, f32[1,1024]{1,0:T(1,128)} %bitcast.11, f32[5,3,5]{2,1,0:T(4,128)} %bitcast.9, f32[5,6,5]{2,1,0:T(8,128)} %bitcast.7, ...), custom_call_target="tpu_custom_call" | custom-call | tf_op jit(solution)/shard_map/pallas_call | solution.py:517
  12.3 1.1 %shard_map.150 = (f32[5,64,1024]{2,1,0:T(8,128)}, f32[128]{0:T(128)}) custom-call(f32[8,5,64,128]{3,2,1,0:T(8,128)S(1)} %get-tuple-element.4.acc_ref, f32[128]{0:T(128)S(1)} %get-tuple-element.5.sums_ref), custom_call_target="tpu_custom_call" | custom-call | tf_op jit(solution)/shard_map/pallas_call | solution.py:548

commit v9 on v7

--- a/solution.py
+++ b/solution.py
@@ -172,11 +172,11 @@
         for h in (1, 2, 3, 0, 4)
         for t in range(tiles)
     }
-    for k in (9, 8, 10):
+    for k in (9, 8, 10, 6):
         loads[k].start()
     for key in fields:
         fields[key].start()
-    for k in (6, 1, 13, 2, 3, 11, 7, 12, 4, 5):
+    for k in (1, 13, 2, 3, 11, 7, 12, 4, 5):
         loads[k].start()
 
     sec = lax.axis_index("sector")
@@ -222,6 +222,11 @@
     up_b = remote(bsend_ref.at[2], brecv_ref.at[0], 4, dev_next)
     down_b = remote(bsend_ref.at[0], brecv_ref.at[1], 5, dev_prev)
 
+    @pl.when(jnp.logical_not(has_high))
+    def _():
+        pl.semaphore_wait(barrier, 4)
+        pl.semaphore_signal(far_sem, inc=1, device_id=dev_next, device_id_type=MESH)
+
     slot_ids = lax.broadcasted_iota(jnp.int32, (1, slots), 1)
     rows_slots = lax.broadcasted_iota(jnp.int32, (elems, slots), 0).astype(jnp.int16)
 
@@ -253,12 +258,24 @@
         for t in range(tiles):
             take_trace(t, face)
         both = dot(tr_ref[face], oh_ref[i])
-        send_ref[i] = both[:80] + both[80:]
+        both = both[:80] + both[80:]
+        if i < 2:
+            send_ref[i] = both
+            return
+        for n in range(0, slots, 128):
+            parts = [both[16 * h : 16 * h + 16, n : n + 128] for h in range(5)]
+            for c in range(5):
+                value = mixed(coef_ref, 9 - face, c, parts)
+                send_ref[i, 16 * c : 16 * c + 16, n : n + 128] = value
 
     for k in (9, 8, 10):
         loads[k].wait()
     for i in range(4):
         find_slots(i)
+    loads[6].wait()
+    for c in range(5):
+        for h in range(5):
+            coef_ref[5 * c + h] = jnp.broadcast_to(0.1 * nbrmat_ref[c][:, h : h + 1], (6, 128))
     for key in fields:
         fields[key].wait()
     def sum_blocks():
@@ -294,8 +311,6 @@
     @pl.when(jnp.logical_not(has_high))
     def _():
         sum_blocks()
-        pl.semaphore_wait(barrier, 4)
-        pl.semaphore_signal(far_sem, inc=1, device_id=dev_next, device_id_type=MESH)
         up_b.start()
         down_b.start()
 
@@ -310,13 +325,11 @@
     def _():
         pl.semaphore_wait(barrier, 3)
 
-    even = axi % 2 == 0
-
-    @pl.when(jnp.logical_and(has_high, even))
+    @pl.when(has_high)
     def _():
         up_z.start()
 
-    @pl.when(jnp.logical_and(has_low, jnp.logical_not(even)))
+    @pl.when(has_low)
     def _():
         down_z.start()
 
@@ -333,14 +346,6 @@
     up_x.start()
     down_x.start()
 
-    @pl.when(jnp.logical_and(has_high, jnp.logical_not(even)))
-    def _():
-        up_z.start()
-
-    @pl.when(jnp.logical_and(has_low, even))
-    def _():
-        down_z.start()
-
     @pl.when(has_high)
     def _():
         sum_blocks()
@@ -350,11 +355,8 @@
     def _():
         down_b.start()
 
-    for k in (7, 12, 4, 5, 6):
+    for k in (7, 12, 4, 5):
         loads[k].wait()
-    for c in range(5):
-        for h in range(5):
-            coef_ref[5 * c + h] = jnp.broadcast_to(0.1 * nbrmat_ref[c][:, h : h + 1], (6, 128))
     for i in range(4):
         find_places(i)
 
@@ -413,19 +415,18 @@
             parts = [both[16 * h : 16 * h + 16, 128 * t : 128 * t + 128] for h in range(5)]
             add_face(acc_ref, t, f, [mixed(coef_ref, f, c, parts) for c in range(5)])
 
-    gather(2)
-    gather(3)
-
-    @pl.when(jnp.logical_not(has_low))
-    def _():
-        pl.semaphore_wait(far_sem, 1)
-        down_b.start()
-
+    for f in (2, 3, 4, 5):
+        gather(f)
     up_x.wait()
     down_x.wait()
     gather(0, 0)
     gather(1, 1)
 
+    @pl.when(jnp.logical_not(has_low))
+    def _():
+        pl.semaphore_wait(far_sem, 1)
+        down_b.start()
+
     @pl.when(has_high)
     def _():
         up_z.wait_send()
@@ -436,8 +437,13 @@
         down_z.wait_send()
         up_z.wait_recv()
 
-    gather(4, 2)
-    gather(5, 3)
+    for i in (2, 3):
+        both = dot(jnp.concatenate(split2(recv_ref[i]), axis=0), place_ref[i])
+        both = both[:80] + both[80:]
+        for t in range(tiles):
+            lanes = slice(128 * t, 128 * t + 128)
+            rows = [both[16 * c : 16 * c + 16, lanes] for c in range(5)]
+            add_face(acc_ref, t, SIDES[i], rows)
 
     up_b.wait()
     down_b.wait()

time: 13.4 us -> 12.7 us (0.948)
  the two profiles are of different devices: /device:TPU:0 before, /device:TPU:27 now
where the time goes in v9:
time: 12.7 us; the launch traced here: 12.5 us
  Pallas kernels  11.9 us (94%)
  between operations  0.64 us (5%)
    pallas_call x1, Pallas kernels, on_device(): pl.pallas_call(functools.partial(exchange, sectors, slabs, owned), out_sh...  10.8 us
    pallas_call x1, Pallas kernels, on_device(): pl.pallas_call(finish, out_shape=(jax.ShapeDtypeStruct(adjoint.shape, F32...  1.13 us

profile of v9, /device:TPU:27, one launch (start us, length us, event | category | flops | bytes accessed | tf_op | source)
XLA Modules:
  0.0 12.5 jit_solution(10924619010966166927)
XLA Ops:
  0.6 10.8 %shard_map.149 = (f32[8,5,64,128]{3,2,1,0:T(8,128)S(1)}, f32[128]{0:T(128)S(1)}) custom-call(f32[5,64,1024]{2,1,0:T(8,128)} %refs_0_.1, bf16[3,64,1024]{2,1,0:T(8,128)(2,1)} %refs_1_.1, f32[1,1024]{1,0:T(1,128)} %bitcast.10, f32[1,1024]{1,0:T(1,128)} %bitcast.11, f32[5,3,5]{2,1,0:T(4,128)} %bitcast.9, f32[5,6,5]{2,1,0:T(8,128)} %bitcast.7, ...), custom_call_target="tpu_custom_call" | custom-call | tf_op jit(solution)/shard_map/pallas_call | solution.py:504
  11.4 1.1 %shard_map.150 = (f32[5,64,1024]{2,1,0:T(8,128)}, f32[128]{0:T(128)}) custom-call(f32[8,5,64,128]{3,2,1,0:T(8,128)S(1)} %get-tuple-element.4.acc_ref, f32[128]{0:T(128)S(1)} %get-tuple-element.5.sums_ref), custom_call_target="tpu_custom_call" | custom-call | tf_op jit(solution)/shard_map/pallas_call | solution.py:535

commit v10 on v9

--- a/solution.py
+++ b/solution.py
@@ -172,13 +172,6 @@
         for h in (1, 2, 3, 0, 4)
         for t in range(tiles)
     }
-    for k in (9, 8, 10, 6):
-        loads[k].start()
-    for key in fields:
-        fields[key].start()
-    for k in (1, 13, 2, 3, 11, 7, 12, 4, 5):
-        loads[k].start()
-
     sec = lax.axis_index("sector")
     axi = lax.axis_index("axial")
     joint = sec * slabs + axi
@@ -192,6 +185,26 @@
     has_low = axi > 0
     has_high = axi < slabs - 1
 
+    def start_block_loads():
+        for k in (1, 13, 2, 3, 11):
+            loads[k].start()
+
+    @pl.when(jnp.logical_not(has_high))
+    def _():
+        start_block_loads()
+
+    for k in (9, 8, 10, 6):
+        loads[k].start()
+    for key in fields:
+        fields[key].start()
+
+    @pl.when(has_high)
+    def _():
+        start_block_loads()
+
+    for k in (7, 12, 4, 5):
+        loads[k].start()
+
     barrier = pltpu.get_barrier_semaphore()
 
     def greet(device):
@@ -222,62 +235,6 @@
     up_b = remote(bsend_ref.at[2], brecv_ref.at[0], 4, dev_next)
     down_b = remote(bsend_ref.at[0], brecv_ref.at[1], 5, dev_prev)
 
-    @pl.when(jnp.logical_not(has_high))
-    def _():
-        pl.semaphore_wait(barrier, 4)
-        pl.semaphore_signal(far_sem, inc=1, device_id=dev_next, device_id_type=MESH)
-
-    slot_ids = lax.broadcasted_iota(jnp.int32, (1, slots), 1)
-    rows_slots = lax.broadcasted_iota(jnp.int32, (elems, slots), 0).astype(jnp.int16)
-
-    columns = lax.broadcasted_iota(jnp.int32, (slots, elems), 1).astype(jnp.int16)
-
-    def slot_row(i):
-        if i >= 2:
-            return aslots_ref[i - 2 : i - 1, :]
-        return jnp.where(slot_ids < live_ref[:, i : i + 1], sslots_ref[i : i + 1, :], -1)
-
-    def find_slots(i):
-        ids = jnp.broadcast_to(slot_row(i), (elems, slots)).astype(jnp.int16)
-        oh_ref[i] = one_hot(rows_slots == ids)
-
-    def find_places(i):
-        ids = jnp.broadcast_to(slot_row(i), (128, slots)).T
-        ids = jnp.concatenate([ids] * tiles, axis=1).astype(jnp.int16)
-        place_ref[i] = one_hot(columns == ids)
-
-    def take_trace(t, face):
-        lanes = slice(128 * t, 128 * t + 128)
-        for c in range(5):
-            hi, lo = split2(face_rows(x_ref, t, c, face))
-            tr_ref[face, 16 * c : 16 * c + 16, lanes] = hi
-            tr_ref[face, 80 + 16 * c : 96 + 16 * c, lanes] = lo
-
-    def fill_send(i):
-        face = SIDES[i]
-        for t in range(tiles):
-            take_trace(t, face)
-        both = dot(tr_ref[face], oh_ref[i])
-        both = both[:80] + both[80:]
-        if i < 2:
-            send_ref[i] = both
-            return
-        for n in range(0, slots, 128):
-            parts = [both[16 * h : 16 * h + 16, n : n + 128] for h in range(5)]
-            for c in range(5):
-                value = mixed(coef_ref, 9 - face, c, parts)
-                send_ref[i, 16 * c : 16 * c + 16, n : n + 128] = value
-
-    for k in (9, 8, 10):
-        loads[k].wait()
-    for i in range(4):
-        find_slots(i)
-    loads[6].wait()
-    for c in range(5):
-        for h in range(5):
-            coef_ref[5 * c + h] = jnp.broadcast_to(0.1 * nbrmat_ref[c][:, h : h + 1], (6, 128))
-    for key in fields:
-        fields[key].wait()
     def sum_blocks():
         for k in (1, 13, 2, 3, 11):
             loads[k].wait()
@@ -301,19 +258,85 @@
         rel = eb_ref[...] - (joint - 1) * owned
         rel = jnp.where(rel < 0, rel + BLOCKS, rel)
         rel = jnp.where(rel >= BLOCKS, rel - BLOCKS, rel)
-        rows_blk = lax.broadcasted_iota(jnp.int32, (width, elems), 0).astype(jnp.int16)
+        for j in (1, 0):
+            rel = jnp.where(rel >= owned * (j + 1), rel + (width - owned), rel)
+        rows_blk = lax.broadcasted_iota(jnp.int32, (3 * width, elems), 0).astype(jnp.int16)
+        ids = jnp.broadcast_to(rel, (3 * width, elems)).astype(jnp.int16)
+        sums = dot_nt(stack, one_hot(rows_blk == ids))
+        total = jnp.sum(sums, axis=0, keepdims=True)
         for j in range(3):
-            ids = jnp.broadcast_to(rel - j * owned, (width, elems)).astype(jnp.int16)
-            sums = dot_nt(stack, one_hot(rows_blk == ids))
-            total = jnp.sum(sums, axis=0, keepdims=True)
-            bsend_ref[j] = jnp.broadcast_to(total, (8, width))
+            part = total[:, j * width : (j + 1) * width]
+            bsend_ref[j] = jnp.broadcast_to(part, (8, width))
 
     @pl.when(jnp.logical_not(has_high))
     def _():
+        pl.semaphore_wait(barrier, 4)
+        pl.semaphore_signal(far_sem, inc=1, device_id=dev_next, device_id_type=MESH)
+        for h in (1, 2, 3):
+            for t in range(tiles):
+                fields[t, h].wait()
         sum_blocks()
         up_b.start()
         down_b.start()
 
+    slot_ids = lax.broadcasted_iota(jnp.int32, (1, slots), 1)
+    rows_slots = lax.broadcasted_iota(jnp.int32, (elems, slots), 0).astype(jnp.int16)
+
+    columns = lax.broadcasted_iota(jnp.int32, (slots, elems), 1).astype(jnp.int16)
+
+    def slot_row(i):
+        if i >= 2:
+            return aslots_ref[i - 2 : i - 1, :]
+        return jnp.where(slot_ids < live_ref[:, i : i + 1], sslots_ref[i : i + 1, :], -1)
+
+    def find_slots(i):
+        ids = jnp.broadcast_to(slot_row(i), (elems, slots)).astype(jnp.int16)
+        oh_ref[i] = one_hot(rows_slots == ids)
+
+    def find_places(i):
+        ids = jnp.broadcast_to(slot_row(i), (128, slots)).T
+        ids = jnp.concatenate([ids] * tiles, axis=1).astype(jnp.int16)
+        place_ref[i] = one_hot(columns == ids)
+
+    def take_trace(t, face):
+        lanes = slice(128 * t, 128 * t + 128)
+        for c in range(5):
+            hi, lo = split2(face_rows(x_ref, t, c, face))
+            tr_ref[face, 16 * c : 16 * c + 16, lanes] = hi
+            tr_ref[face, 80 + 16 * c : 96 + 16 * c, lanes] = lo
+
+    def fill_send(i):
+        face = SIDES[i]
+        for t in range(tiles):
+            take_trace(t, face)
+        both = dot(tr_ref[face], oh_ref[i])
+        both = both[:80] + both[80:]
+        if i < 2:
+            send_ref[i] = both
+            return
+        for n in range(0, slots, 128):
+            parts = [both[16 * h : 16 * h + 16, n : n + 128] for h in range(5)]
+            for c in range(5):
+                value = mixed(coef_ref, 9 - face, c, parts)
+                send_ref[i, 16 * c : 16 * c + 16, n : n + 128] = value
+
+    for k in (9, 8, 10):
+        loads[k].wait()
+    for i in range(4):
+        find_slots(i)
+    loads[6].wait()
+    for c in range(5):
+        for h in range(5):
+            coef_ref[5 * c + h] = jnp.broadcast_to(0.1 * nbrmat_ref[c][:, h : h + 1], (6, 128))
+    @pl.when(has_high)
+    def _():
+        for h in (1, 2, 3):
+            for t in range(tiles):
+                fields[t, h].wait()
+
+    for h in (0, 4):
+        for t in range(tiles):
+            fields[t, h].wait()
     fill_send(2)
     fill_send(3)
 
@@ -420,12 +443,13 @@
     up_x.wait()
     down_x.wait()
     gather(0, 0)
-    gather(1, 1)
 
     @pl.when(jnp.logical_not(has_low))
     def _():
         pl.semaphore_wait(far_sem, 1)
         down_b.start()
+
+    gather(1, 1)
 
     @pl.when(has_high)
     def _():

time: 12.7 us -> 12.2 us (0.961)
  Pallas kernels: 11.9 us -> 11.4 us
    pallas_call x1, Pallas kernels: 10.8 us -> 10.2 us  [on_device(): pl.pallas_call(functools.partial(exchange, sectors, slabs, owned), out_sh...]
where the time goes in v10:
time: 12.2 us; the launch traced here: 12 us
  Pallas kernels  11.4 us (93%)
  between operations  0.64 us (5%)
    pallas_call x1, Pallas kernels, on_device(): pl.pallas_call(functools.partial(exchange, sectors, slabs, owned), out_sh...  10.2 us
    pallas_call x1, Pallas kernels, on_device(): pl.pallas_call(finish, out_shape=(jax.ShapeDtypeStruct(adjoint.shape, F32...  1.13 us

profile of v10, /device:TPU:27, one launch (start us, length us, event | category | flops | bytes accessed | tf_op | source)
XLA Modules:
  0.0 12.0 jit_solution(9102137038023294333)
XLA Ops:
  0.6 10.2 %shard_map.149 = (f32[8,5,64,128]{3,2,1,0:T(8,128)S(1)}, f32[128]{0:T(128)S(1)}) custom-call(f32[5,64,1024]{2,1,0:T(8,128)} %refs_0_.1, bf16[3,64,1024]{2,1,0:T(8,128)(2,1)} %refs_1_.1, f32[1,1024]{1,0:T(1,128)} %bitcast.10, f32[1,1024]{1,0:T(1,128)} %bitcast.11, f32[5,3,5]{2,1,0:T(4,128)} %bitcast.9, f32[5,6,5]{2,1,0:T(8,128)} %bitcast.7, ...), custom_call_target="tpu_custom_call" | custom-call | tf_op jit(solution)/shard_map/pallas_call | solution.py:528
  10.9 1.1 %shard_map.150 = (f32[5,64,1024]{2,1,0:T(8,128)}, f32[128]{0:T(128)}) custom-call(f32[8,5,64,128]{3,2,1,0:T(8,128)S(1)} %get-tuple-element.4.acc_ref, f32[128]{0:T(128)S(1)} %get-tuple-element.5.sums_ref), custom_call_target="tpu_custom_call" | custom-call | tf_op jit(solution)/shard_map/pallas_call | solution.py:559

commit v11 on v10

--- a/solution.py
+++ b/solution.py
@@ -185,6 +185,19 @@
     has_low = axi > 0
     has_high = axi < slabs - 1
 
+    barrier = pltpu.get_barrier_semaphore()
+
+    def greet(device):
+        pl.semaphore_signal(barrier, inc=1, device_id=device, device_id_type=MESH)
+
+    greet(dev_low)
+    greet(dev_high)
+    greet(dev_prev)
+
+    @pl.when(has_high)
+    def _():
+        greet(dev_next)
+
     def start_block_loads():
         for k in (1, 13, 2, 3, 11):
             loads[k].start()
@@ -204,19 +217,6 @@
 
     for k in (7, 12, 4, 5):
         loads[k].start()
-
-    barrier = pltpu.get_barrier_semaphore()
-
-    def greet(device):
-        pl.semaphore_signal(barrier, inc=1, device_id=device, device_id_type=MESH)
-
-    greet(dev_low)
-    greet(dev_high)
-    greet(dev_prev)
-
-    @pl.when(has_high)
-    def _():
-        greet(dev_next)
 
     def remote(src, dst, k, device):
         return pltpu.make_async_remote_copy(
@@ -440,15 +440,15 @@
 
     for f in (2, 3, 4, 5):
         gather(f)
+
+    @pl.when(jnp.logical_not(has_low))
+    def _():
+        pl.semaphore_wait(far_sem, 1)
+        down_b.start()
+
     up_x.wait()
     down_x.wait()
     gather(0, 0)
-
-    @pl.when(jnp.logical_not(has_low))
-    def _():
-        pl.semaphore_wait(far_sem, 1)
-        down_b.start()
-
     gather(1, 1)
 
     @pl.when(has_high)

time: 12.2 us -> 12.1 us (level)
  the two profiles are of different devices: /device:TPU:27 before, /device:TPU:0 now
where the time goes in v11:
time: 12.1 us; the launch traced here: 11.9 us
  Pallas kernels  11.3 us (93%)
  between operations  0.64 us (5%)
    pallas_call x1, Pallas kernels, on_device(): pl.pallas_call(functools.partial(exchange, sectors, slabs, owned), out_sh...  10.1 us
    pallas_call x1, Pallas kernels, on_device(): pl.pallas_call(finish, out_shape=(jax.ShapeDtypeStruct(adjoint.shape, F32...  1.13 us

profile of v11, /device:TPU:0, one launch (start us, length us, event | category | flops | bytes accessed | tf_op | source)
XLA Modules:
  0.0 11.9 jit_solution(1758432365897189078)
XLA Ops:
  0.6 10.1 %shard_map.149 = (f32[8,5,64,128]{3,2,1,0:T(8,128)S(1)}, f32[128]{0:T(128)S(1)}) custom-call(f32[5,64,1024]{2,1,0:T(8,128)} %refs_0_.1, bf16[3,64,1024]{2,1,0:T(8,128)(2,1)} %refs_1_.1, f32[1,1024]{1,0:T(1,128)} %bitcast.10, f32[1,1024]{1,0:T(1,128)} %bitcast.11, f32[5,3,5]{2,1,0:T(4,128)} %bitcast.9, f32[5,6,5]{2,1,0:T(8,128)} %bitcast.7, ...), custom_call_target="tpu_custom_call" | custom-call | tf_op jit(solution)/shard_map/pallas_call | solution.py:528
  10.8 1.1 %shard_map.150 = (f32[5,64,1024]{2,1,0:T(8,128)}, f32[128]{0:T(128)}) custom-call(f32[8,5,64,128]{3,2,1,0:T(8,128)S(1)} %get-tuple-element.4.acc_ref, f32[128]{0:T(128)S(1)} %get-tuple-element.5.sums_ref), custom_call_target="tpu_custom_call" | custom-call | tf_op jit(solution)/shard_map/pallas_call | solution.py:559

commit v12 on v11

--- a/solution.py
+++ b/solution.py
@@ -169,8 +169,8 @@
         (t, h): pltpu.make_async_copy(
             hbm_refs[0].at[h, :, pl.ds(128 * t, 128)], x_ref.at[t, h], x_sem.at[5 * t + h]
         )
-        for h in (1, 2, 3, 0, 4)
         for t in range(tiles)
+        for h in range(5)
     }
     sec = lax.axis_index("sector")
     axi = lax.axis_index("axial")
@@ -202,14 +202,24 @@
         for k in (1, 13, 2, 3, 11):
             loads[k].start()
 
+    def start_fields(*which):
+        for t in range(tiles):
+            for h in which:
+                fields[t, h].start()
+
     @pl.when(jnp.logical_not(has_high))
     def _():
         start_block_loads()
+        start_fields(1, 2, 3)
 
     for k in (9, 8, 10, 6):
         loads[k].start()
-    for key in fields:
-        fields[key].start()
+
+    @pl.when(has_high)
+    def _():
+        start_fields(1, 2, 3)
+
+    start_fields(0, 4)
 
     @pl.when(has_high)
     def _():
@@ -235,12 +245,15 @@
     up_b = remote(bsend_ref.at[2], brecv_ref.at[0], 4, dev_next)
     down_b = remote(bsend_ref.at[0], brecv_ref.at[1], 5, dev_prev)
 
-    def sum_blocks():
+    def sum_blocks(arriving):
         for k in (1, 13, 2, 3, 11):
             loads[k].wait()
         parts = []
         for t in range(tiles):
             lanes = slice(128 * t, 128 * t + 128)
+            if arriving:
+                for h in (1, 2, 3):
+                    fields[t, h].wait()
             total = x_ref[t, 1] * vel_ref[0, :, lanes].astype(F32)
             total += x_ref[t, 2] * vel_ref[1, :, lanes].astype(F32)
             total += x_ref[t, 3] * vel_ref[2, :, lanes].astype(F32)
@@ -272,10 +285,7 @@
     def _():
         pl.semaphore_wait(barrier, 4)
         pl.semaphore_signal(far_sem, inc=1, device_id=dev_next, device_id_type=MESH)
-        for h in (1, 2, 3):
-            for t in range(tiles):
-                fields[t, h].wait()
-        sum_blocks()
+        sum_blocks(True)
         up_b.start()
         down_b.start()
 
@@ -371,7 +381,7 @@
 
     @pl.when(has_high)
     def _():
-        sum_blocks()
+        sum_blocks(False)
         up_b.start()
 
     @pl.when(jnp.logical_and(has_low, has_high))
@@ -438,18 +448,23 @@
             parts = [both[16 * h : 16 * h + 16, 128 * t : 128 * t + 128] for h in range(5)]
             add_face(acc_ref, t, f, [mixed(coef_ref, f, c, parts) for c in range(5)])
 
-    for f in (2, 3, 4, 5):
-        gather(f)
-
-    @pl.when(jnp.logical_not(has_low))
-    def _():
-        pl.semaphore_wait(far_sem, 1)
-        down_b.start()
+    def answer_far(mine):
+        @pl.when(jnp.logical_and(jnp.logical_not(has_low), mine))
+        def _():
+            pl.semaphore_wait(far_sem, 1)
+            down_b.start()
+
+    gather(2)
+    gather(3)
+    gather(4)
+    answer_far(sec >= sectors // 2)
+    gather(5)
 
     up_x.wait()
     down_x.wait()
     gather(0, 0)
     gather(1, 1)
+    answer_far(sec < sectors // 2)
 
     @pl.when(has_high)
     def _():

time: 12.1 us -> 12.5 us (1.033)
  Pallas kernels: 11.3 us -> 11.7 us
    pallas_call x1, Pallas kernels: 10.1 us -> 10.5 us  [on_device(): pl.pallas_call(functools.partial(exchange, sectors, slabs, owned), out_sh...]
where the time goes in v12:
time: 12.5 us; the launch traced here: 12.3 us
  Pallas kernels  11.7 us (94%)
  between operations  0.64 us (5%)
    pallas_call x1, Pallas kernels, on_device(): pl.pallas_call(functools.partial(exchange, sectors, slabs, owned), out_sh...  10.5 us
    pallas_call x1, Pallas kernels, on_device(): pl.pallas_call(finish, out_shape=(jax.ShapeDtypeStruct(adjoint.shape, F32...  1.13 us

profile of v12, /device:TPU:0, one launch (start us, length us, event | category | flops | bytes accessed | tf_op | source)
XLA Modules:
  0.0 12.3 jit_solution(5195873246734548632)
XLA Ops:
  0.6 10.5 %shard_map.149 = (f32[8,5,64,128]{3,2,1,0:T(8,128)S(1)}, f32[128]{0:T(128)S(1)}) custom-call(f32[5,64,1024]{2,1,0:T(8,128)} %refs_0_.1, bf16[3,64,1024]{2,1,0:T(8,128)(2,1)} %refs_1_.1, f32[1,1024]{1,0:T(1,128)} %bitcast.10, f32[1,1024]{1,0:T(1,128)} %bitcast.11, f32[5,3,5]{2,1,0:T(4,128)} %bitcast.9, f32[5,6,5]{2,1,0:T(8,128)} %bitcast.7, ...), custom_call_target="tpu_custom_call" | custom-call | tf_op jit(solution)/shard_map/pallas_call | solution.py:543
  11.2 1.1 %shard_map.150 = (f32[5,64,1024]{2,1,0:T(8,128)}, f32[128]{0:T(128)}) custom-call(f32[8,5,64,128]{3,2,1,0:T(8,128)S(1)} %get-tuple-element.4.acc_ref, f32[128]{0:T(128)S(1)} %get-tuple-element.5.sums_ref), custom_call_target="tpu_custom_call" | custom-call | tf_op jit(solution)/shard_map/pallas_call | solution.py:574

commit v13 on v11

--- a/solution.py
+++ b/solution.py
@@ -147,6 +147,7 @@
         recv_ref,
         a_ref,
         coef_ref,
+        blocks_ref,
         bsend_ref,
         brecv_ref,
         send_sem,
@@ -199,8 +200,10 @@
         greet(dev_next)
 
     def start_block_loads():
-        for k in (1, 13, 2, 3, 11):
+        for k in (1, 13, 2, 3):
             loads[k].start()
+
+    loads[11].start()
 
     @pl.when(jnp.logical_not(has_high))
     def _():
@@ -235,8 +238,19 @@
     up_b = remote(bsend_ref.at[2], brecv_ref.at[0], 4, dev_next)
     down_b = remote(bsend_ref.at[0], brecv_ref.at[1], 5, dev_prev)
 
+    loads[11].wait()
+    rel = eb_ref[...] - (joint - 1) * owned
+    rel = jnp.where(rel < 0, rel + BLOCKS, rel)
+    rel = jnp.where(rel >= BLOCKS, rel - BLOCKS, rel)
+    for j in (1, 0):
+        rel = jnp.where(rel >= owned * (j + 1), rel + (width - owned), rel)
+    ids = jnp.broadcast_to(rel, (128, elems)).T.astype(jnp.int16)
+    for j in range(3 * width // 128):
+        lanes = lax.broadcasted_iota(jnp.int32, (elems, 128), 1) + 128 * j
+        blocks_ref[:, 128 * j : 128 * j + 128] = one_hot(lanes.astype(jnp.int16) == ids)
+
     def sum_blocks():
-        for k in (1, 13, 2, 3, 11):
+        for k in (1, 13, 2, 3):
             loads[k].wait()
         parts = []
         for t in range(tiles):
@@ -255,14 +269,7 @@
         stack = jnp.where(row16 == 0, w1.astype(F32), 0.0)
         stack = jnp.where(row16 == 1, w2.astype(F32), stack)
         stack = jnp.where(row16 == 2, w3, stack).astype(BF)
-        rel = eb_ref[...] - (joint - 1) * owned
-        rel = jnp.where(rel < 0, rel + BLOCKS, rel)
-        rel = jnp.where(rel >= BLOCKS, rel - BLOCKS, rel)
-        for j in (1, 0):
-            rel = jnp.where(rel >= owned * (j + 1), rel + (width - owned), rel)
-        rows_blk = lax.broadcasted_iota(jnp.int32, (3 * width, elems), 0).astype(jnp.int16)
-        ids = jnp.broadcast_to(rel, (3 * width, elems)).astype(jnp.int16)
-        sums = dot_nt(stack, one_hot(rows_blk == ids))
+        sums = dot(stack, blocks_ref[...])
         total = jnp.sum(sums, axis=0, keepdims=True)
         for j in range(3):
             part = total[:, j * width : (j + 1) * width]
@@ -438,17 +445,19 @@
             parts = [both[16 * h : 16 * h + 16, 128 * t : 128 * t + 128] for h in range(5)]
             add_face(acc_ref, t, f, [mixed(coef_ref, f, c, parts) for c in range(5)])
 
+    def answer_far(mine):
+        @pl.when(jnp.logical_and(jnp.logical_not(has_low), mine))
+        def _():
+            pl.semaphore_wait(far_sem, 1)
+            down_b.start()
+
     for f in (2, 3, 4, 5):
         gather(f)
-
-    @pl.when(jnp.logical_not(has_low))
-    def _():
-        pl.semaphore_wait(far_sem, 1)
-        down_b.start()
-
+    answer_far(sec >= sectors // 2)
     up_x.wait()
     down_x.wait()
     gather(0, 0)
+    answer_far(sec < sectors // 2)
     gather(1, 1)
 
     @pl.when(has_high)
@@ -544,6 +553,7 @@
             pltpu.VMEM((4, 80, slots), F32),
             pltpu.VMEM((320, 1024), BF),
             pltpu.VMEM((25, 6, 128), F32),
+            pltpu.VMEM((elems, 3 * width), BF),
             pltpu.VMEM((3, 8, width), F32),
             pltpu.VMEM((2, 8, width), F32),
             pltpu.SemaphoreType.DMA((6,)),

time: 12.1 us -> 12 us (level)
  no operation moved by 1% of the time
where the time goes in v13:
time: 12 us; the launch traced here: 11.9 us
  Pallas kernels  11.2 us (93%)
  between operations  0.64 us (5%)
    pallas_call x1, Pallas kernels, on_device(): pl.pallas_call(functools.partial(exchange, sectors, slabs, owned), out_sh...  10.1 us
    pallas_call x1, Pallas kernels, on_device(): pl.pallas_call(finish, out_shape=(jax.ShapeDtypeStruct(adjoint.shape, F32...  1.13 us

profile of v13, /device:TPU:0, one launch (start us, length us, event | category | flops | bytes accessed | tf_op | source)
XLA Modules:
  0.0 11.9 jit_solution(3574139683078053653)
XLA Ops:
  0.6 10.1 %shard_map.149 = (f32[8,5,64,128]{3,2,1,0:T(8,128)S(1)}, f32[128]{0:T(128)S(1)}) custom-call(f32[5,64,1024]{2,1,0:T(8,128)} %refs_0_.1, bf16[3,64,1024]{2,1,0:T(8,128)(2,1)} %refs_1_.1, f32[1,1024]{1,0:T(1,128)} %bitcast.10, f32[1,1024]{1,0:T(1,128)} %bitcast.11, f32[5,3,5]{2,1,0:T(4,128)} %bitcast.9, f32[5,6,5]{2,1,0:T(8,128)} %bitcast.7, ...), custom_call_target="tpu_custom_call" | custom-call | tf_op jit(solution)/shard_map/pallas_call | solution.py:537
  10.7 1.1 %shard_map.150 = (f32[5,64,1024]{2,1,0:T(8,128)}, f32[128]{0:T(128)}) custom-call(f32[8,5,64,128]{3,2,1,0:T(8,128)S(1)} %get-tuple-element.4.acc_ref, f32[128]{0:T(128)S(1)} %get-tuple-element.5.sums_ref), custom_call_target="tpu_custom_call" | custom-call | tf_op jit(solution)/shard_map/pallas_call | solution.py:569

commit v14 on v11

--- a/solution.py
+++ b/solution.py
@@ -348,13 +348,13 @@
     def _():
         pl.semaphore_wait(barrier, 3)
 
+    @pl.when(has_low)
+    def _():
+        down_z.start()
+
     @pl.when(has_high)
     def _():
         up_z.start()
-
-    @pl.when(has_low)
-    def _():
-        down_z.start()
 
     @pl.when(jnp.logical_not(has_low))
     def _():

time: 12.1 us -> 12.1 us (level)
  no operation moved by 1% of the time
where the time goes in v14:
time: 12.1 us; the launch traced here: 11.9 us
  Pallas kernels  11.3 us (93%)
  between operations  0.64 us (5%)
    pallas_call x1, Pallas kernels, on_device(): pl.pallas_call(functools.partial(exchange, sectors, slabs, owned), out_sh...  10.1 us
    pallas_call x1, Pallas kernels, on_device(): pl.pallas_call(finish, out_shape=(jax.ShapeDtypeStruct(adjoint.shape, F32...  1.13 us

profile of v14, /device:TPU:0, one launch (start us, length us, event | category | flops | bytes accessed | tf_op | source)
XLA Modules:
  0.0 11.9 jit_solution(12159903086038235681)
XLA Ops:
  0.6 10.1 %shard_map.149 = (f32[8,5,64,128]{3,2,1,0:T(8,128)S(1)}, f32[128]{0:T(128)S(1)}) custom-call(f32[5,64,1024]{2,1,0:T(8,128)} %refs_0_.1, bf16[3,64,1024]{2,1,0:T(8,128)(2,1)} %refs_1_.1, f32[1,1024]{1,0:T(1,128)} %bitcast.10, f32[1,1024]{1,0:T(1,128)} %bitcast.11, f32[5,3,5]{2,1,0:T(4,128)} %bitcast.9, f32[5,6,5]{2,1,0:T(8,128)} %bitcast.7, ...), custom_call_target="tpu_custom_call" | custom-call | tf_op jit(solution)/shard_map/pallas_call | solution.py:528
  10.8 1.1 %shard_map.150 = (f32[5,64,1024]{2,1,0:T(8,128)}, f32[128]{0:T(128)}) custom-call(f32[8,5,64,128]{3,2,1,0:T(8,128)S(1)} %get-tuple-element.4.acc_ref, f32[128]{0:T(128)S(1)} %get-tuple-element.5.sums_ref), custom_call_target="tpu_custom_call" | custom-call | tf_op jit(solution)/shard_map/pallas_call | solution.py:559
